TPU v7x, 128 devices: a whole 4x4x4 slice. The times are simulated.
128 devices in a mesh: pole: 8 (over x, y_lo), grid: 16 (over z, y_hi, core).
Axes of the slice: x: 4, y: 4 (y_hi: 2, y_lo: 2; y = y_hi * 2 + y_lo), z: 4, core: 2. Of those that a mesh axis runs over, the one named last changes fastest.
Arguments:
- hamiltonian: float32 [2048, 2048], P(('pole', 'grid')), may hold values from -6 to 6, as said below
- margin: float32 [2048, 2048], P(('pole', 'grid')), may hold values from -1 to 1.2, as said below
- pattern: int32 [4, 4], replicated, may hold values 0 or 1
- shift_real: float32 [8], P('pole'), may hold values from -0.5 to 0.5
- shift_imag: float32 [8], P('pole'), may hold values from 0.3 to 3
- residue: float32 [8, 2], P('pole'), may hold values from -4 to 4
Outputs:
- density: float32 [2048, 2048], P(('pole', 'grid'))
Inputs may be any that keep to these rules, and one draw needn't show every extreme that they name: `hamiltonian`: symmetric. `margin`: symmetric.
All inputs are finite; a program needn't handle non-finite values.
Results may differ from a plain program's by a relative error of at most 0.0003.
Values sent between devices are 32-bit elements; how exact they have to be, the bound alone decides.
A program may use at most 320 MiB of HBM per device.

v0:
```python
from functools import partial

import jax
import jax.numpy as jnp
from jax import lax
from jax.sharding import PartitionSpec as P

SUPER = 256
NC = 2
NR = 4
C = 512
R = 1024


HIGH = lax.Precision.HIGHEST


def ceinsum(form, left, right):
    mult = partial(jnp.einsum, form, precision=HIGH, preferred_element_type=jnp.float32)
    return (
        mult(left[0], right[0]) - mult(left[1], right[1]),
        mult(left[0], right[1]) + mult(left[1], right[0]),
    )


def cmul(left, right):
    return (left[0] * right[0] - left[1] * right[1], left[0] * right[1] + left[1] * right[0])


def fold_term(lhs, piece, start):
    batch, height, width = lhs[0].shape
    blocks = piece[0].shape[1]
    count = piece[0].shape[2]

    def cut(part):
        return lax.dynamic_slice_in_dim(
            part.reshape(batch, height, blocks, width // blocks), start, count, 3
        )

    return ceinsum("xaqj,xqjc->xac", (cut(lhs[0]), cut(lhs[1])), piece)


def folder(lhs, carry, piece, start):
    term = fold_term(lhs, piece, start)
    return (carry[0] + term[0], carry[1] + term[1])


def zero_pair(shape):
    empty = jnp.zeros(shape, jnp.float32)
    return (empty, empty)


def flatten(pair):
    batch, blocks, rows, width = pair[0].shape
    return (
        pair[0].reshape(batch, blocks * rows, width),
        pair[1].reshape(batch, blocks * rows, width),
    )


def newton(matrix):
    real, imag = matrix
    batch, blocks, rows, width = real.shape
    whole_real, whole_imag = (
        lax.all_gather(real, "grid", axis=2, tiled=True),
        lax.all_gather(imag, "grid", axis=2, tiled=True),
    )
    whole = (whole_real.reshape(batch, width, width), whole_imag.reshape(batch, width, width))
    diag_real = jnp.diagonal(whole[0], axis1=1, axis2=2)
    diag_imag = jnp.diagonal(whole[1], axis1=1, axis2=2)
    denom = diag_real * diag_real + diag_imag * diag_imag
    inv_real = diag_real / denom
    inv_imag = -diag_imag / denom
    scaled = cmul((inv_real[:, :, None], inv_imag[:, :, None]), whole)
    scaled = cmul(scaled, (inv_real[:, None, :], inv_imag[:, None, :]))
    eye = jnp.eye(width, dtype=jnp.float32)
    start_full = (
        2.0 * eye * inv_real[:, None, :] - scaled[0],
        2.0 * eye * inv_imag[:, None, :] - scaled[1],
    )
    grid_count = lax.axis_size("grid")

    def own_rows(part):
        split = part.reshape(batch, blocks, grid_count, rows, width)
        return lax.dynamic_index_in_dim(split, lax.axis_index("grid"), 2, keepdims=False).reshape(
            batch, blocks * rows, width
        )

    start_rows = (own_rows(start_full[0]), own_rows(start_full[1]))
    product = ceinsum("xak,xkc->xac", start_rows, whole)
    second = ceinsum("xak,xkc->xac", product, start_full)
    return (
        (2.0 * start_rows[0] - second[0]).reshape(real.shape),
        (2.0 * start_rows[1] - second[1]).reshape(real.shape),
    )


def local(hamiltonian, margin, pattern, shift_real, shift_imag, residue):
    grid_count = lax.axis_size("grid")
    offset = lax.axis_index("grid") * hamiltonian.shape[0]
    rows = hamiltonian.shape[0]
    width = hamiltonian.shape[1]
    ham_all, over_all = (
        lax.all_gather(hamiltonian[None], "pole", axis=0, tiled=True),
        lax.all_gather(margin[None], "pole", axis=0, tiled=True),
    )
    blocks_all = ham_all.shape[0]
    span = rows * grid_count
    child_blocks = C // span
    root_blocks = R // span
    global_rows = jnp.arange(blocks_all)[:, None] * span + offset + jnp.arange(rows)[None, :]
    columns = jnp.arange(width)
    pattern_float = pattern.astype(jnp.float32)
    row_child = global_rows < 2 * C
    col_child = columns < 2 * C
    same_child = (
        row_child[:, :, None]
        & col_child[None, None, :]
        & ((global_rows // C)[:, :, None] == (columns // C)[None, None, :])
    )
    both_root = jnp.logical_not(row_child)[:, :, None] & jnp.logical_not(col_child)[None, None, :]
    root_hot = (((global_rows - 2 * C) // SUPER)[:, :, None] == jnp.arange(NR)).astype(jnp.float32)
    child_hot_col = ((columns // SUPER)[:, None] == jnp.arange(2 * NC)[None, :]).astype(jnp.float32)
    upper = jnp.dot(jnp.dot(root_hot, pattern_float), child_hot_col.T)
    child_hot_row = ((global_rows // SUPER)[:, :, None] == jnp.arange(2 * NC)).astype(jnp.float32)
    root_hot_col = (((columns - 2 * C) // SUPER)[:, None] == jnp.arange(NR)[None, :]).astype(
        jnp.float32
    )
    lower = jnp.dot(jnp.dot(child_hot_row, pattern_float.T), root_hot_col.T)
    mask = same_child.astype(jnp.float32) + both_root.astype(jnp.float32) + upper + lower
    total = jnp.zeros((blocks_all, rows, width), jnp.float32)
    real = (ham_all - shift_real[0] * over_all) * mask
    imag = -shift_imag[0] * over_all * mask

    def kids(part):
        return jnp.stack(
            [
                part[k * child_blocks : (k + 1) * child_blocks, :, k * C : (k + 1) * C]
                for k in (0, 1)
            ]
        )

    def kid_cross(part):
        return jnp.stack(
            [part[k * child_blocks : (k + 1) * child_blocks, :, 2 * C :] for k in (0, 1)]
        )

    def root_cross(part):
        return jnp.stack([part[2 * child_blocks :, :, k * C : (k + 1) * C] for k in (0, 1)])

    kid_inv = newton((kids(real), kids(imag)))
    kid_flat = flatten(kid_inv)
    couple_rows = flatten((root_cross(real), root_cross(imag)))
    factor = folder(
        couple_rows,
        zero_pair((2, root_blocks * rows, C)),
        (
            lax.all_gather(kid_inv[0], "grid", axis=2, tiled=True),
            lax.all_gather(kid_inv[1], "grid", axis=2, tiled=True),
        ),
        jnp.int32(0),
    )
    schur = folder(
        factor,
        zero_pair((2, root_blocks * rows, R)),
        (
            lax.all_gather(kid_cross(real), "grid", axis=2, tiled=True),
            lax.all_gather(kid_cross(imag), "grid", axis=2, tiled=True),
        ),
        jnp.int32(0),
    )
    root_real = real[2 * child_blocks :, :, 2 * C :].reshape(1, root_blocks * rows, R)
    root_imag = imag[2 * child_blocks :, :, 2 * C :].reshape(1, root_blocks * rows, R)
    reduced_real = root_real - schur[0][0:1] - schur[0][1:2]
    reduced_imag = root_imag - schur[1][0:1] - schur[1][1:2]
    root_shape = (1, root_blocks, rows, R)
    root_inv = newton((reduced_real.reshape(root_shape), reduced_imag.reshape(root_shape)))
    root_flat = flatten(root_inv)
    factor_shape = (2, root_blocks, rows, C)
    full_real = lax.all_gather(factor[0].reshape(factor_shape), "grid", axis=2, tiled=True)
    full_imag = lax.all_gather(factor[1].reshape(factor_shape), "grid", axis=2, tiled=True)
    full_factor = (full_real.reshape(2, R, C), full_imag.reshape(2, R, C))
    upward = ceinsum("ak,xkc->xac", (root_flat[0][0], root_flat[1][0]), full_factor)
    panel_out = (-upward[0], -upward[1])

    def split_cols(part):
        return part.reshape(2, root_blocks, rows, child_blocks, grid_count, rows)

    moved_real = lax.all_to_all(
        split_cols(panel_out[0]), "grid", split_axis=4, concat_axis=4, tiled=True
    )
    moved_imag = lax.all_to_all(
        split_cols(panel_out[1]), "grid", split_axis=4, concat_axis=4, tiled=True
    )

    def reorder(part):
        return jnp.transpose(part, (0, 3, 5, 1, 4, 2)).reshape(2, child_blocks * rows, R)

    side = (reorder(moved_real), reorder(moved_imag))
    kid_term = ceinsum("xak,xkc->xac", side, full_factor)
    weight_real = residue[0, 0]
    weight_imag = residue[0, 1]

    def weigh(first, second):
        return weight_real * first - weight_imag * second

    diag_part = weigh(kid_flat[0] - kid_term[0], kid_flat[1] - kid_term[1])
    side_part = weigh(side[0], side[1])
    panel_part = weigh(panel_out[0], panel_out[1])
    root_part = weigh(root_flat[0], root_flat[1])
    empty = jnp.zeros((child_blocks * rows, C), jnp.float32)
    first_rows = jnp.concatenate([diag_part[0], empty, side_part[0]], axis=1).reshape(
        child_blocks, rows, width
    )
    second_rows = jnp.concatenate([empty, diag_part[1], side_part[1]], axis=1).reshape(
        child_blocks, rows, width
    )
    third_rows = jnp.concatenate([panel_part[0], panel_part[1], root_part[0]], axis=1).reshape(
        root_blocks, rows, width
    )
    total = total + jnp.concatenate([first_rows, second_rows, third_rows], axis=0)
    total = total * mask
    whole_sum = lax.psum(total, "pole")
    return lax.dynamic_index_in_dim(whole_sum, lax.axis_index("pole"), 0, keepdims=False)


def solution(mesh):
    return jax.shard_map(
        local,
        mesh=mesh,
        in_specs=(
            P(("pole", "grid"), None),
            P(("pole", "grid"), None),
            P(),
            P("pole"),
            P("pole"),
            P("pole", None),
        ),
        out_specs=P(("pole", "grid"), None),
        check_vma=False,
    )
```

profile of v0, /device:TPU:1, one launch (start us, length us, event | category | flops | bytes accessed | tf_op | source)
XLA Modules:
  0.0 900.5 jit_solution(13454485038826729235)
XLA Ops:
  12.0 34.7 %all-gather.35.cloned.1.call-done = f32[128,2048]{1,0:T(8,128)} async-done(((f32[16,2048]{1,0:T(8,128)}), f32[128,2048]{1,0:T(8,128)}) %all-gather.35.cloned.1.call-update) | async-done | bytes 1048592 | tf_op jit(solution)/shard_map/all_gather | solution.py:104
  46.7 40.1 %all-gather.37.cloned.1.call-done = f32[128,2048]{1,0:T(8,128)} async-done(((f32[16,2048]{1,0:T(8,128)}), f32[128,2048]{1,0:T(8,128)}) %all-gather.37.cloned.1.call-update) | async-done | bytes 1048592 | tf_op jit(solution)/shard_map/all_gather | solution.py:105
  94.6 51.0 %all-gather.15.cloned.1.call-done = f32[2,2,256,512]{3,2,1,0:T(8,128)} async-done(((f32[2,2,16,512]{3,2,1,0:T(8,128)}), f32[2,2,256,512]{3,2,1,0:T(8,128)}) %all-gather.15.cloned.1.call-update) | async-done | bytes 2097168 | tf_op jit(solution)/shard_map/all_gather | solution.py:65
  145.6 61.1 %copy.87 = f32[2,512,512]{0,2,1:T(8,128)} copy(f32[2,512,512]{2,1,0:T(8,128)} %bitcast.249) | data formatting | bytes 4194304 | tf_op jit(solution)/shard_map/reshape | solution.py:68
  206.7 5.5 gather_fusion
  212.4 61.2 %copy.89 = f32[2,512,512]{0,2,1:T(8,128)} copy(f32[2,512,512]{2,1,0:T(8,128)} %bitcast.253) | data formatting | bytes 4194304 | tf_op jit(solution)/shard_map/reshape | solution.py:68
  273.6 5.5 gather_fusion.1
  302.1 36.5 %all-gather.19.cloned.1.call-done = f32[2,2,256,512]{3,2,1,0:T(8,128)} async-done(((f32[2,2,16,512]{3,2,1,0:T(8,128)}), f32[2,2,256,512]{3,2,1,0:T(8,128)}) %all-gather.19.cloned.1.call-update) | async-done | bytes 2097168 | tf_op jit(solution)/shard_map/all_gather | solution.py:158
  341.6 45.7 %all-gather.21.cloned.1.call-done = f32[2,2,256,512]{3,2,1,0:T(8,128)} async-done(((f32[2,2,16,512]{3,2,1,0:T(8,128)}), f32[2,2,256,512]{3,2,1,0:T(8,128)}) %all-gather.21.cloned.1.call-update) | async-done | bytes 2097168 | tf_op jit(solution)/shard_map/all_gather | solution.py:159
  394.1 49.9 %all-gather.25.cloned.1.call-done = f32[2,2,256,1024]{3,2,1,0:T(8,128)} async-done(((f32[2,2,16,1024]{3,2,1,0:T(8,128)}), f32[2,2,256,1024]{3,2,1,0:T(8,128)}) %all-gather.25.cloned.1.call-update) | async-done | bytes 4194320 | tf_op jit(solution)/shard_map/all_gather | solution.py:167
  444.0 4.8 convolution_bitcast_fusion.3
  450.3 49.4 %all-gather.27.cloned.1.call-done = f32[2,2,256,1024]{3,2,1,0:T(8,128)} async-done(((f32[2,2,16,1024]{3,2,1,0:T(8,128)}), f32[2,2,256,1024]{3,2,1,0:T(8,128)}) %all-gather.27.cloned.1.call-update) | async-done | bytes 4194320 | tf_op jit(solution)/shard_map/all_gather | solution.py:168
  499.7 4.8 fusion.4
  506.6 5.0 convolution_bitcast_fusion.1
  519.6 39.0 %all-gather.29.cloned.1.call-done = f32[1,4,256,1024]{3,2,1,0:T(8,128)} async-done(((f32[1,4,16,1024]{3,2,1,0:T(8,128)}), f32[1,4,256,1024]{3,2,1,0:T(8,128)}) %all-gather.29.cloned.1.call-update) | async-done | bytes 4194320 | tf_op jit(solution)/shard_map/all_gather | solution.py:65
  558.6 17.6 %gather_fusion.2 = f32[1024]{0:T(1024)S(1)} fusion(f32[1024,1024]{1,0:T(8,128)} %bitcast.233, s32[1024]{0:T(1024)S(1)} %bitcast.229), kind=kCustom, calls=%fused_computation.2 | custom fusion | bytes 16384 | tf_op jit(solution)/shard_map/jit(diagonal)/gather | solution.py:69
  576.2 37.9 %all-gather.31.cloned.1.call-done = f32[1,4,256,1024]{3,2,1,0:T(8,128)} async-done(((f32[1,4,16,1024]{3,2,1,0:T(8,128)}), f32[1,4,256,1024]{3,2,1,0:T(8,128)}) %all-gather.31.cloned.1.call-update) | async-done | bytes 4194320 | tf_op jit(solution)/shard_map/all_gather | solution.py:66
  614.1 17.4 %gather_fusion.3 = f32[1024]{0:T(1024)S(1)} fusion(f32[1024,1024]{1,0:T(8,128)} %bitcast.237, s32[1024]{0:T(1024)S(1)} %bitcast.230), kind=kCustom, calls=%fused_computation.3 | custom fusion | bytes 16384 | tf_op jit(solution)/shard_map/jit(diagonal)/gather | solution.py:70
  631.8 4.2 multiply_subtract_fusion.1
  656.9 12.9 %all-gather.23.cloned.1.call-done = f32[2,4,256,512]{3,2,1,0:T(8,128)} async-done(((f32[2,4,16,512]{3,2,1,0:T(8,128)}), f32[2,4,256,512]{3,2,1,0:T(8,128)}) %all-gather.23.cloned.1.call-update) | async-done | bytes 4194320 | tf_op jit(solution)/shard_map/all_gather | solution.py:180
  669.8 5.1 fusion.40
  674.8 5.6 fusion.26
  680.4 44.9 %all-gather.33.cloned.1.call-done = f32[2,4,256,512]{3,2,1,0:T(8,128)} async-done(((f32[2,4,16,512]{3,2,1,0:T(8,128)}), f32[2,4,256,512]{3,2,1,0:T(8,128)}) %all-gather.33.cloned.1.call-update) | async-done | bytes 4194320 | tf_op jit(solution)/shard_map/all_gather | solution.py:181
  725.3 5.2 fusion.38
  730.5 7.1 multiply_subtract_fusion.5
  748.7 4.5 all-to-all-start
  753.2 6.8 multiply_subtract_fusion.6
  763.2 5.0 reshape.1035
  768.9 7.3 all-to-all-start.1
  788.6 4.8 fusion.116
  808.2 5.4 fusion.17
  818.0 74.2 %all-reduce.2.cloned.1.call-done = f32[8,16,2048]{2,1,0:T(8,128)} async-done(((f32[8,16,2048]{2,1,0:T(8,128)}), f32[8,16,2048]{2,1,0:T(8,128)}) %all-reduce.2.cloned.1.call-update) | async-done | bytes 1048592 | tf_op jit(solution)/shard_map/psum | solution.py:223
  (191 shorter events, 124.4 us)
Async XLA Ops:
  6.5 82.1 %copy-start.27 = (s32[4,4]{1,0:T(4,128)S(1)}, s32[4,4]{1,0:T(4,128)}, u32[]{:S(2)}) copy-start(s32[4,4]{1,0:T(4,128)} %param.8) | copy-start | bytes 196
  6.5 40.2 %all-gather.35.cloned.1.call-start = ((), (), s32[]{:S(2)}) async-start(), calls=%async_computation.13 | async-start | bytes 1179648 | tf_op jit(solution)/shard_map/all_gather | solution.py:104
  7.3 79.6 %all-gather.37.cloned.1.call-start = ((), (), s32[]{:S(2)}) async-start(), calls=%async_computation.14 | async-start | bytes 1179648 | tf_op jit(solution)/shard_map/all_gather | solution.py:105
  8.0 137.6 %all-gather.15.cloned.1.call-start = ((), (), s32[]{:S(2)}) async-start(), calls=%async_computation.2 | async-start | bytes 2228224 | tf_op jit(solution)/shard_map/all_gather | solution.py:65
  93.5 118.9 %all-gather.17.cloned.1.call-start = ((), (), s32[]{:S(2)}) async-start(), calls=%async_computation.3 | async-start | bytes 2228224 | tf_op jit(solution)/shard_map/all_gather | solution.py:66
  94.2 244.4 %all-gather.19.cloned.1.call-start = ((), (), s32[]{:S(2)}) async-start(), calls=%async_computation.4 | async-start | bytes 2228224 | tf_op jit(solution)/shard_map/all_gather | solution.py:158
  212.4 67.2 %copy-start.9 = (f32[2,2,256,512]{3,2,1,0:T(8,128)S(1)}, f32[2,2,256,512]{3,2,1,0:T(8,128)}, u32[]{:S(2)}) copy-start(f32[2,2,256,512]{3,2,1,0:T(8,128)} %all-gather.15.cloned.1.call-done) | copy-start | bytes 6291460
  290.1 9.1 %copy-start.20 = (f32[8,16,2048]{2,1,0:T(8,128)S(1)}, f32[8,16,2048]{2,1,0:T(8,128)}, u32[]{:S(2)}) copy-start(f32[8,16,2048]{2,1,0:T(8,128)} %get-tuple-element.27) | copy-start | bytes 3145732
  290.2 9.9 %copy-start.19 = (f32[8,16,2048]{2,1,0:T(8,128)S(1)}, f32[8,16,2048]{2,1,0:T(8,128)}, u32[]{:S(2)}) copy-start(f32[8,16,2048]{2,1,0:T(8,128)} %copy-done.18) | copy-start | bytes 3145732
  292.2 95.2 %all-gather.21.cloned.1.call-start = ((), (), s32[]{:S(2)}) async-start(), calls=%async_computation.5 | async-start | bytes 2228224 | tf_op jit(solution)/shard_map/all_gather | solution.py:159
  299.1 144.9 %all-gather.25.cloned.1.call-start = ((), (), s32[]{:S(2)}) async-start(), calls=%async_computation.7 | async-start | bytes 4456448 | tf_op jit(solution)/shard_map/all_gather | solution.py:167
  300.0 199.7 %all-gather.27.cloned.1.call-start = ((), (), s32[]{:S(2)}) async-start(), calls=%async_computation.8 | async-start | bytes 4456448 | tf_op jit(solution)/shard_map/all_gather | solution.py:168
  300.8 257.8 %all-gather.29.cloned.1.call-start = ((), (), s32[]{:S(2)}) async-start(), calls=%async_computation.9 | async-start | bytes 4456448 | tf_op jit(solution)/shard_map/all_gather | solution.py:65
  391.0 57.8 %copy-start.14 = (f32[2,2,256,512]{3,2,1,0:T(8,128)S(1)}, f32[2,2,256,512]{3,2,1,0:T(8,128)}, u32[]{:S(2)}) copy-start(f32[2,2,256,512]{3,2,1,0:T(8,128)} %all-gather.19.cloned.1.call-done) | copy-start | bytes 6291460
  394.1 112.5 %copy-start.16 = (f32[2,64,512]{2,1,0:T(8,128)}, f32[2,64,512]{2,1,0:T(8,128)S(1)}, u32[]{:S(2)}) copy-start(f32[2,64,512]{2,1,0:T(8,128)S(1)} %fusion.12) | copy-start | bytes 786436
  450.3 61.4 %copy-start.17 = (f32[2,64,512]{2,1,0:T(8,128)}, f32[2,64,512]{2,1,0:T(8,128)S(1)}, u32[]{:S(2)}) copy-start(f32[2,64,512]{2,1,0:T(8,128)S(1)} %fusion.11) | copy-start | bytes 786436
  450.3 54.2 %copy-start.24 = (f32[4,16,1024]{2,1,0:T(8,128)S(1)}, f32[4,16,1024]{2,1,0:T(8,128)}, u32[]{:S(2)}) copy-start(f32[4,16,1024]{2,1,0:T(8,128)} %slice.120) | copy-start | bytes 786436
  505.3 108.8 %all-gather.31.cloned.1.call-start = ((), (), s32[]{:S(2)}) async-start(), calls=%async_computation.10 | async-start | bytes 4456448 | tf_op jit(solution)/shard_map/all_gather | solution.py:66
  505.5 6.2 copy-start.13
  515.1 154.6 %all-gather.23.cloned.1.call-start = ((), (), s32[]{:S(2)}) async-start(), calls=%async_computation.6 | async-start | bytes 4456448 | tf_op jit(solution)/shard_map/all_gather | solution.py:180
  515.8 209.4 %all-gather.33.cloned.1.call-start = ((), (), s32[]{:S(2)}) async-start(), calls=%async_computation.11 | async-start | bytes 4456448 | tf_op jit(solution)/shard_map/all_gather | solution.py:181
  631.8 5.4 copy-start.5
  730.5 7.1 copy-start.6
  748.7 20.2 %all-to-all-start = ((f32[16,1,4096]{2,1,0:T(1,128)}), f32[16,1,4096]{2,1,0:T(1,128)}, u32[]{:S(2)}, u32[]{:S(2)}) async-start(f32[16,1,4096]{2,1,0:T(1,128)} %reshape.1037), calls=%async_computation | async-start | bytes 524288 | tf_op jit(solution)/shard_map/all_to_all | solution.py:189
  760.1 8.1 copy-start.23
  768.9 27.0 %all-to-all-start.1 = ((f32[16,1,4096]{2,1,0:T(1,128)}), f32[16,1,4096]{2,1,0:T(1,128)S(1)}, u32[]{:S(2)}, u32[]{:S(2)}) async-start(f32[16,1,4096]{2,1,0:T(1,128)} %reshape.1035), calls=%async_computation.1 | async-start | bytes 524288 | tf_op jit(solution)/shard_map/all_to_all | solution.py:192
  776.2 116.0 %all-reduce.2.cloned.1.call-start = ((), (), s32[]{:S(2)}) async-start(), calls=%async_computation.12 | async-start | bytes 2097152 | tf_op jit(solution)/shard_map/psum | solution.py:223
  801.4 6.8 copy-start.21
  805.1 8.5 copy-start.22
  806.7 7.0 copy-start.8
  808.2 8.6 copy-start.15
  808.2 8.6 copy-start.26
  (12 other events, 46.5 us)
Sparse Core Ops, SparseCore 0:
  9.0 37.6 all-gather.34
  48.4 38.4 all-gather.36
  93.6 51.9 all-gather.14
  148.0 46.3 all-gather.16
  292.3 46.3 all-gather.18
  341.0 46.3 all-gather.20
  389.8 54.1 all-gather.24
  446.5 53.1 all-gather.26
  505.4 53.1 all-gather.28
  560.9 53.1 all-gather.30
  616.6 53.1 all-gather.22
  672.1 53.1 all-gather.32
  818.1 74.0 all-reduce.1
where the time goes:
time: 919 us; the launch traced here: 900 us
  waiting for transfers between devices  519 us (56%)
  local copies, waits for them, and re-layouts  212 us (23%)
  matrix products  115 us (13%)
  other arithmetic  26.6 us (3%)
  between operations  15.7 us (2%)
  starting transfers between devices  12.9 us (1%)
    all_gather x2, waiting for transfers between devices, newton(): lax.all_gather(real, 'grid', axis=2, tiled=True)  90.1 us
    psum x1, waiting for transfers between devices, local(): whole_sum = lax.psum(total, 'pole')  74.2 us
    reshape x1, local copies, waits for them, and re-layouts, newton(): whole_imag.reshape(batch, width, width)  61.2 us
    reshape x1, local copies, waits for them, and re-layouts, newton(): whole_real.reshape(batch, width, width)  61.1 us
    all_gather x1, waiting for transfers between devices, local(): lax.all_gather(kid_cross(real), 'grid', axis=2, tiled=True)  49.9 us
    all_gather x1, waiting for transfers between devices, local(): lax.all_gather(kid_cross(imag), 'grid', axis=2, tiled=True)  49.4 us
    all_gather x1, waiting for transfers between devices, local(): lax.all_gather(kid_inv[1], 'grid', axis=2, tiled=True)  45.7 us
    all_gather x1, waiting for transfers between devices, local(): lax.all_gather(factor[1].reshape(factor_shape), 'grid', axis=2, tiled=True)  44.9 us
  transfers between devices with their start and end apart: 15, of which 12 were waited for; matrix products, arithmetic and copies ran while one was open for 24% of the time, Pallas kernels for 0%

commit v1 on v0

v1 whole, which is shorter than its diff:
```python
import jax
import jax.numpy as jnp
from jax import lax
from jax.experimental import pallas as pl
from jax.experimental.pallas import tpu as pltpu
from jax.sharding import PartitionSpec as P

C = 512
R = 1024
F32 = jnp.float32
BF16 = jnp.bfloat16
MESH = pl.DeviceIdType.MESH
ANY = pl.BlockSpec(memory_space=pl.ANY)
VM = pl.BlockSpec(memory_space=pltpu.VMEM)
SM = pl.BlockSpec(memory_space=pltpu.SMEM)
BLOCKS = ((0, 0), (0, 1), (0, 2), (1, 1), (1, 2), (1, 3), (2, 2), (2, 3), (3, 3), (3, 0))
NB = len(BLOCKS)


def mod4(v):
    return lax.rem(v + 4, 4)


def half(v):
    return lax.div(v, 2)


def place():
    p = lax.axis_index("pole")
    g = lax.axis_index("grid")
    x, yl = half(p), lax.rem(p, 2)
    z, q, c = lax.div(g, 4), half(g), lax.rem(g, 2)
    return p, g, x, yl, z, lax.rem(q, 2), q, c


def spot(x, y, z, c):
    return (2 * x + lax.rem(y, 2), 4 * z + 2 * half(y) + c)


def greet(devices):
    barrier = pltpu.get_barrier_semaphore()
    for device in devices:
        pl.semaphore_signal(barrier, inc=1, device_id=device, device_id_type=MESH)
    pl.semaphore_wait(barrier, len(devices))


def remote(src, dst, send, recv, device):
    return pltpu.make_async_remote_copy(
        src_ref=src, dst_ref=dst, send_sem=send, recv_sem=recv, device_id=device, device_id_type=MESH
    )


def gather_kernel(
    h_ref, s_ref, ab_ref, a0_ref,
    loc_sem, sib_s, sib_r, x_s, x_r, f_s, f_r, fo_s, fo_r, g_s, g_r, go_s, go_r,
    y0_s, y0_r, x0_s, x0_r,
):
    p, g, x, yl, z, yh, q, c = place()
    y = 2 * yh + yl
    sibling = (p, g + 1 - 2 * c)
    partner = (p + 1 - 2 * yl, g)
    xs = [spot(mod4(x + d), y, z, c) for d in (1, 2, 3)]
    ys = [spot(x, mod4(y + d), z, c) for d in (1, -1)]
    zs = [spot(x, y, mod4(z + d), c) for d in (1, -1)]
    greet([sibling] + xs + ys + zs)
    first = c == 0

    def pick(a, b):
        return tuple(jnp.where(first, u, v) for u, v in zip(a, b))

    fs = [pick(ys[i], zs[i]) for i in (0, 1)]
    gs = [pick(zs[i], ys[i]) for i in (0, 1)]
    f0 = jnp.where(first, y, z)
    g0 = jnp.where(first, z, y)

    def row(slot, f, s):
        yy, zz = jnp.where(first, f, s), jnp.where(first, s, f)
        return pl.multiple_of(slot * 512 + lax.rem(yy, 2) * 256 + (2 * zz + half(yy)) * 32, 32)

    def slab(slot, f, s):
        return ab_ref.at[:, pl.ds(row(slot, f, s), 32), :]

    def part(slot, f, s, k):
        return ab_ref.at[k, pl.ds(row(slot, f, s), 32), :]

    root = x >= 2
    mine = jnp.logical_or(root, x == c)
    his = jnp.logical_or(root, x == 1 - c)
    slot0 = jnp.maximum(x - 1, 0)
    row0 = pl.multiple_of(slot0 * 512 + yl * 256 + q * 32 + c * 16, 16)
    inputs = (h_ref, s_ref)
    own_cols = pl.ds(pl.multiple_of(c * 512, 128), 512)
    sib_cols = pl.ds(pl.multiple_of((1 - c) * 512, 128), 512)
    dst_rows = pl.ds(row0, 16)
    sib_rows = pl.ds(pl.multiple_of(row0 + (1 - 2 * c) * 16, 16), 16)
    own = [pltpu.make_async_copy(inputs[k].at[:, own_cols], ab_ref.at[k, dst_rows, :], loc_sem.at[k]) for k in (0, 1)]
    to_sib = [
        remote(inputs[k].at[:, sib_cols], ab_ref.at[k, dst_rows, :], sib_s.at[k], sib_r.at[k], sibling)
        for k in (0, 1)
    ]
    from_sib = [
        remote(inputs[k].at[:, own_cols], ab_ref.at[k, sib_rows, :], sib_s.at[k], sib_r.at[k], sibling)
        for k in (0, 1)
    ]
    j0 = 2 * jnp.maximum(x - 2, 0) + yl
    j1 = 2 * jnp.maximum(x - 2, 0) + 1 - yl

    def top(k, j):
        return a0_ref.at[k, pl.ds(pl.multiple_of(j * 16, 16), 16), :]

    top_src = [inputs[k].at[:, pl.ds(1024, 1024)] for k in (0, 1)]
    top_own = [pltpu.make_async_copy(top_src[k], top(k, j0), loc_sem.at[2 + k]) for k in (0, 1)]
    top_y = [remote(top_src[k], top(k, j0), y0_s.at[k], y0_r.at[k], partner) for k in (0, 1)]
    top_y_in = [remote(top_src[k], top(k, j1), y0_s.at[k], y0_r.at[k], partner) for k in (0, 1)]
    sx = jnp.maximum(x - 2, 0)
    top_x = [
        remote(top_src[k], top(k, j0), x0_s.at[n, 0, k], x0_r.at[sx, 0, k], xs[n]) for n in range(3) for k in (0, 1)
    ]
    top_x2 = [
        remote(top(k, j1), top(k, j1), x0_s.at[n, 1, k], x0_r.at[sx, 1, k], xs[n]) for n in range(3) for k in (0, 1)
    ]

    @pl.when(mine)
    def _():
        for copy in own:
            copy.start()

    @pl.when(his)
    def _():
        for copy in to_sib:
            copy.start()

    @pl.when(root)
    def _():
        for copy in top_y:
            copy.start()

    @pl.when(mine)
    def _():
        for copy in own:
            copy.wait()
        for copy in from_sib:
            copy.wait_recv()

    to_x = [remote(slab(slot0, f0, g0), slab(slot0, f0, g0), x_s.at[n], x_r.at[slot0], xs[n]) for n in range(3)]

    @pl.when(mine)
    def _():
        for copy in to_x:
            copy.start()

    @pl.when(root)
    def _():
        for copy in top_own:
            copy.start()
        for copy in top_x:
            copy.start()

    for slot in range(3):
        not_mine = jnp.logical_or(jnp.logical_not(mine), slot0 != slot)

        @pl.when(not_mine)
        def _():
            remote(slab(slot, f0, g0), slab(slot, f0, g0), x_s.at[0], x_r.at[slot], xs[0]).wait_recv()

    pending = []

    def go(copy):
        copy.start()
        pending.append(copy)

    f_at = (mod4(f0 - 1), mod4(f0 + 1), mod4(f0 + 2))
    g_at = (mod4(g0 - 1), mod4(g0 + 1), mod4(g0 + 2))
    for slot in range(3):
        for d in (0, 1):
            ref = slab(slot, f0, g0)
            go(remote(ref, ref, f_s.at[d, slot], f_r.at[d, slot], fs[d]))

    def spread(slot, n, f):
        ref = slab(slot, f, g0)
        for d in (0, 1):
            go(remote(ref, ref, g_s.at[d, slot, n], g_r.at[d, slot, n], gs[d]))

    for slot in range(3):
        spread(slot, 0, f0)
    for slot in range(3):
        for d in (0, 1):
            ref = slab(slot, f_at[d], g0)
            remote(ref, ref, f_s.at[d, slot], f_r.at[d, slot], fs[d]).wait_recv()
            ref = part(slot, f_at[d], g0, d)
            go(remote(ref, ref, fo_s.at[slot, d], fo_r.at[slot, d], fs[d]))
            spread(slot, 1 + d, f_at[d])

    @pl.when(root)
    def _():
        for k in (0, 1):
            top_y_in[k].wait_recv()
        for copy in top_x2:
            copy.start()

    def relay(slot, n, f):
        for d in (0, 1):
            ref = slab(slot, f, g_at[d])
            remote(ref, ref, g_s.at[d, slot, n], g_r.at[d, slot, n], gs[d]).wait_recv()
            ref = part(slot, f, g_at[d], d)
            go(remote(ref, ref, go_s.at[slot, n, d], go_r.at[slot, n, d], gs[d]))

    for slot in range(3):
        relay(slot, 0, f0)
    for slot in range(3):
        for d in (0, 1):
            ref = part(slot, f_at[2], g0, d)
            remote(ref, ref, fo_s.at[slot, d], fo_r.at[slot, d], fs[d]).wait_recv()
        spread(slot, 3, f_at[2])
    for n in (1, 2, 3):
        for slot in range(3):
            relay(slot, n, f_at[n - 1])
    for n in range(4):
        f = (f0,) + f_at
        for slot in range(3):
            for d in (0, 1):
                ref = part(slot, f[n], g_at[2], d)
                remote(ref, ref, go_s.at[slot, n, d], go_r.at[slot, n, d], gs[d]).wait_recv()

    for sx_in in (0, 1):
        jx = (2 * sx_in + yl, 2 * sx_in + 1 - yl)

        @pl.when(x != 2 + sx_in)
        def _():
            for o in (0, 1):
                for k in (0, 1):
                    ref = top(k, jx[o])
                    remote(ref, ref, x0_s.at[0, o, k], x0_r.at[sx_in, o, k], xs[0]).wait_recv()

    for copy in pending:
        copy.wait_send()

    @pl.when(his)
    def _():
        for copy in to_sib:
            copy.wait_send()

    @pl.when(mine)
    def _():
        for copy in to_x:
            copy.wait_send()

    @pl.when(root)
    def _():
        for copy in top_own:
            copy.wait()
        for copy in top_y + top_x + top_x2:
            copy.wait_send()


def gather_inputs(ham, margin):
    dma = pltpu.SemaphoreType.DMA
    return pl.pallas_call(
        gather_kernel,
        name="gather_inputs",
        out_shape=(
            jax.ShapeDtypeStruct((2, 1536, 512), F32),
            jax.ShapeDtypeStruct((2, 64, 1024), F32),
        ),
        in_specs=[ANY, ANY],
        out_specs=(ANY, ANY),
        scratch_shapes=[
            dma((4,)), dma((2,)), dma((2,)), dma((3,)), dma((3,)),
            dma((2, 3)), dma((2, 3)), dma((3, 2)), dma((3, 2)),
            dma((2, 3, 4)), dma((2, 3, 4)), dma((3, 4, 2)), dma((3, 4, 2)),
            dma((2,)), dma((2,)), dma((3, 2, 2)), dma((2, 2, 2)),
        ],
        compiler_params=pltpu.CompilerParams(collective_id=0, has_side_effects=True),
        cost_estimate=pl.CostEstimate(flops=0, bytes_accessed=16 << 20, transcendentals=0),
    )(ham, margin)


def split(v):
    high = v.astype(BF16)
    return high, (v - high.astype(F32)).astype(BF16)


def put_pair(lhs_ref, vr, vi):
    m, k = vr.shape
    rh, rl = split(vr)
    ih, il = split(vi)
    for at, (re, im) in enumerate(((rh, ih), (rl, il))):
        base = at * 2 * m
        lhs_ref[base : base + m, 0:k] = re
        lhs_ref[base : base + m, k : 2 * k] = -im
        lhs_ref[base + m : base + 2 * m, 0:k] = im
        lhs_ref[base + m : base + 2 * m, k : 2 * k] = re


def fold(wide, narrow, m):
    total = wide[0 : 2 * m] + wide[2 * m : 4 * m] + narrow
    return total[0:m], total[m : 2 * m]


def dot(a, b):
    return jnp.dot(a, b, preferred_element_type=F32)


def dot_t(a, b):
    return lax.dot_general(a, b, (((1,), (1,)), ((), ())), preferred_element_type=F32)


def times(lhs_ref, rhs_ref, out_ref, vr, vi, width):
    m, k = vr.shape
    put_pair(lhs_ref, vr, vi)
    for n in range(width // 256):
        cols = slice(n * 256, n * 256 + 256)
        wide = dot(lhs_ref[0 : 4 * m, 0 : 2 * k], rhs_ref[0, :, cols])
        narrow = dot(lhs_ref[0 : 2 * m, 0 : 2 * k], rhs_ref[1, :, cols])
        re, im = fold(wide, narrow, m)
        out_ref[0, 0:m, cols] = re
        out_ref[1, 0:m, cols] = im


def rotate(vr, vi, dr, di):
    return vr * dr - vi * di, vr * di + vi * dr


def recip(dr, di):
    den = dr * dr + di * di
    return dr / den, -di / den


def child_kernel(
    sc_ref, id_ref, ab_ref, mb_ref, ehl_ref, dinv_ref, bhl_ref, tb_ref, w_ref, xc_ref,
    lhs_e, lhs_t, u_ref, t_ref,
):
    sr, si = sc_ref[0], sc_ref[1]
    q = id_ref[0]
    dinv_ref[...] = jnp.zeros_like(dinv_ref)

    def scale_rows(n, _):
        r0 = pl.multiple_of(n * 64, 64)
        rows = pl.ds(r0, 64)
        low = pl.ds(pl.multiple_of(n * 64 + C, 64), 64)
        s = ab_ref[1, rows, :]
        re = ab_ref[0, rows, :] - sr * s
        im = -si * s
        eye = lax.broadcasted_iota(jnp.int32, (64, C), 1) == lax.broadcasted_iota(jnp.int32, (64, C), 0) + r0
        ir, ii = recip(
            jnp.sum(jnp.where(eye, re, 0.0), axis=1, keepdims=True),
            jnp.sum(jnp.where(eye, im, 0.0), axis=1, keepdims=True),
        )
        dinv_ref[0:1, :] += jnp.sum(jnp.where(eye, ir, 0.0), axis=0, keepdims=True)
        dinv_ref[1:2, :] += jnp.sum(jnp.where(eye, ii, 0.0), axis=0, keepdims=True)
        er, ei = rotate(re, im, -ir, -ii)
        for part, value in ((rows, er), (low, ei)):
            high, rest = split(jnp.where(eye, 0.0, value))
            ehl_ref[0, part, :] = high
            ehl_ref[1, part, :] = rest
        return 0

    lax.fori_loop(0, 8, scale_rows, 0)

    def couple(rows, j):
        m = mb_ref[pl.ds(j, 1), :]
        s = ab_ref[1, rows, :] * m
        return ab_ref[0, rows, :] * m - sr * s, -si * s

    def split_rows(n, _):
        re, im = couple(pl.ds(pl.multiple_of(C + n * 64, 64), 64), lax.div(n, 4))
        rows = pl.ds(pl.multiple_of(n * 64, 64), 64)
        for at, value in ((0, re), (C, im)):
            high, rest = split(value)
            bhl_ref[0, rows, at : at + C] = high
            bhl_ref[1, rows, at : at + C] = rest
        return 0

    lax.fori_loop(0, 16, split_rows, 0)

    for j in range(4):
        re, im = couple(pl.ds(pl.multiple_of(C + j * 256 + q * 32, 32), 32), j)
        t_ref[0, j * 32 : j * 32 + 32, :] = re
        t_ref[1, j * 32 : j * 32 + 32, :] = im
    vr, vi = t_ref[0, 0:128, :], t_ref[1, 0:128, :]
    times(lhs_e, ehl_ref, u_ref, vr, vi, C)
    u_ref[0, 0:128, :] += t_ref[0, 0:128, :]
    u_ref[1, 0:128, :] += t_ref[1, 0:128, :]
    for jj in range(2):
        at = pl.multiple_of(jj * 256 + q * 32, 32)
        low = pl.multiple_of(jj * 256 + q * 32 + C, 32)
        eye = lax.broadcasted_iota(jnp.int32, (32, C), 1) == lax.broadcasted_iota(jnp.int32, (32, C), 0) + at
        rows = slice(128 + jj * 32, 160 + jj * 32)
        er = ehl_ref[0, pl.ds(at, 32), :].astype(F32) + ehl_ref[1, pl.ds(at, 32), :].astype(F32)
        ei = ehl_ref[0, pl.ds(low, 32), :].astype(F32) + ehl_ref[1, pl.ds(low, 32), :].astype(F32)
        u_ref[0, rows, :] = jnp.where(eye, 1.0, er)
        u_ref[1, rows, :] = ei
    times(lhs_e, ehl_ref, t_ref, u_ref[0], u_ref[1], C)
    times(lhs_e, ehl_ref, t_ref, t_ref[0], t_ref[1], C)
    lr, li = rotate(u_ref[0] + t_ref[0], u_ref[1] + t_ref[1], dinv_ref[0:1, :], dinv_ref[1:2, :])
    xc_ref[0] = lr[128:192]
    xc_ref[1] = li[128:192]
    put_pair(lhs_t, lr, li)
    for n in range(4):
        rows = slice(n * 256, n * 256 + 256)
        wide = dot_t(lhs_t[...], bhl_ref[0, rows, :])
        narrow = dot_t(lhs_t[0:384, :], bhl_ref[1, rows, :])
        pair = fold(wide, narrow, 192)
        for k in (0, 1):
            w_ref[k, :, rows] = pair[k][128:192]
            for b, (j, other) in enumerate(BLOCKS):
                if other == n:
                    for cc in (0, 1):
                        tb_ref[cc, b, k] = pair[k][j * 32 + cc * 16 : j * 32 + cc * 16 + 16]


def child_part(scalars, ids, ab, mask_b):
    return pl.pallas_call(
        child_kernel,
        name="child_part",
        out_shape=(
            jax.ShapeDtypeStruct((2, 1024, C), BF16),
            jax.ShapeDtypeStruct((8, C), F32),
            jax.ShapeDtypeStruct((2, R, 2 * C), BF16),
            jax.ShapeDtypeStruct((2, NB, 2, 16, 256), F32),
            jax.ShapeDtypeStruct((2, 64, R), F32),
            jax.ShapeDtypeStruct((2, 64, C), F32),
        ),
        in_specs=[SM, SM, VM, VM],
        out_specs=(VM,) * 6,
        scratch_shapes=[
            pltpu.VMEM((768, 1024), BF16), pltpu.VMEM((768, 1024), BF16),
            pltpu.VMEM((2, 192, C), F32), pltpu.VMEM((2, 192, C), F32),
        ],
        compiler_params=pltpu.CompilerParams(vmem_limit_bytes=52 << 20),
        cost_estimate=pl.CostEstimate(flops=4 << 30, bytes_accessed=16 << 20, transcendentals=0),
    )(scalars, ids, ab, mask_b)


def schur_kernel(
    sc_ref, tb_ref, a0_ref, sg_ref,
    tin_ref, own_ref, t_s, t_r, loc_sem, y_s, y_r, z_s, z_r, o_s, o_r, b_s, b_r,
):
    p, g, x, yl, z, yh, q, c = place()
    y = 2 * yh + yl
    sibling = (p, g + 1 - 2 * c)
    over = (p, g + 2 - 4 * yh)
    zs = [spot(x, y, mod4(z + d), c) for d in (1, -1)]
    greet([sibling, over] + zs)
    swap = remote(tb_ref.at[1 - c], tin_ref, t_s, t_r, sibling)
    swap.start()
    sr, si = sc_ref[0], sc_ref[1]
    for b, (j, other) in enumerate(BLOCKS):
        s = a0_ref[1, j * 16 : j * 16 + 16, other * 256 : other * 256 + 256]
        own_ref[b, 0] = a0_ref[0, j * 16 : j * 16 + 16, other * 256 : other * 256 + 256] - sr * s - tb_ref[c, b, 0]
        own_ref[b, 1] = -si * s - tb_ref[c, b, 1]
    swap.wait()
    own_ref[...] = own_ref[...] - tin_ref[...]

    pending = []

    def go(copy):
        copy.start()
        pending.append(copy)

    def whole(gg):
        return sg_ref.at[:, :, gg]

    def part(gg, k):
        return sg_ref.at[:, k, gg]

    go(remote(own_ref, whole(g), y_s, y_r, over))
    for d in (0, 1):
        go(remote(own_ref, whole(g), z_s.at[d, 0], z_r.at[d, 0], zs[d]))
    mine = pltpu.make_async_copy(own_ref, whole(g), loc_sem)
    mine.start()
    for k in (0, 1):
        go(remote(own_ref.at[:, k], part(g, k), b_s.at[0, 0, k], b_r.at[0, 0, k], sibling))
    base = (g, g + 2 - 4 * yh)
    z_at = [4 * (mod4(z + d) - z) for d in (-1, 1, 2)]

    def hand_over(n, o, gg):
        for k in (0, 1):
            go(remote(part(gg, k), part(gg, k), b_s.at[n, o, k], b_r.at[n, o, k], sibling))

    remote(whole(base[1]), whole(base[1]), y_s, y_r, over).wait_recv()
    for d in (0, 1):
        go(remote(whole(base[1]), whole(base[1]), z_s.at[d, 1], z_r.at[d, 1], zs[d]))
    hand_over(0, 1, base[1])
    for o in (0, 1):
        for d in (0, 1):
            gg = base[o] + z_at[d]
            remote(whole(gg), whole(gg), z_s.at[d, o], z_r.at[d, o], zs[d]).wait_recv()
            go(remote(part(gg, d), part(gg, d), o_s.at[o, d], o_r.at[o, d], zs[d]))
            hand_over(1 + d, o, gg)
    for o in (0, 1):
        gg = base[o] + z_at[2]
        for d in (0, 1):
            remote(part(gg, d), part(gg, d), o_s.at[o, d], o_r.at[o, d], zs[d]).wait_recv()
            go(remote(part(gg, d), part(gg, d), b_s.at[3, o, d], b_r.at[3, o, d], sibling))
    for n in range(4):
        for o in (0, 1):
            gg = base[o] + ((0,) + tuple(z_at))[n] + 1 - 2 * c
            for k in (0, 1):
                remote(part(gg, k), part(gg, k), b_s.at[n, o, k], b_r.at[n, o, k], sibling).wait_recv()
    mine.wait()
    for copy in pending:
        copy.wait_send()


def share_schur(scalars, tb, a0):
    dma = pltpu.SemaphoreType.DMA
    return pl.pallas_call(
        schur_kernel,
        name="share_schur",
        out_shape=jax.ShapeDtypeStruct((NB, 2, 16, 16, 256), F32),
        in_specs=[SM, VM, VM],
        out_specs=ANY,
        scratch_shapes=[
            pltpu.VMEM((NB, 2, 16, 256), F32), pltpu.VMEM((NB, 2, 16, 256), F32),
            dma, dma, dma, dma, dma, dma((2, 2)), dma((2, 2)), dma((2, 2)), dma((2, 2)),
            dma((4, 2, 2)), dma((4, 2, 2)),
        ],
        compiler_params=pltpu.CompilerParams(collective_id=1, has_side_effects=True),
        cost_estimate=pl.CostEstimate(flops=0, bytes_accessed=16 << 20, transcendentals=0),
    )(scalars, tb, a0)


def root_kernel(
    sc_ref, id_ref, sg_ref, ehl_ref, dinv_ref, bhl_ref, w_ref, xc_ref, mf_ref,
    dw_ref, fw_ref, ft_ref, gw_ref,
    shl_ref, d0_ref, lhs, u_ref, t_ref, k_ref, ku_ref,
):
    g = id_ref[1]
    wr, wi = sc_ref[2], sc_ref[3]
    where = {pair: b for b, pair in enumerate(BLOCKS)}
    eye = lax.broadcasted_iota(jnp.int32, (256, 256), 1) == lax.broadcasted_iota(jnp.int32, (256, 256), 0)
    for j in range(4):
        rows = slice(j * 256, j * 256 + 256)
        low = slice(R + j * 256, R + j * 256 + 256)
        b = where[(j, j)]
        ir, ii = recip(
            jnp.sum(jnp.where(eye, sg_ref[b, 0], 0.0), axis=1, keepdims=True),
            jnp.sum(jnp.where(eye, sg_ref[b, 1], 0.0), axis=1, keepdims=True),
        )
        d0_ref[0:1, rows] = jnp.sum(jnp.where(eye, ir, 0.0), axis=0, keepdims=True)
        d0_ref[1:2, rows] = jnp.sum(jnp.where(eye, ii, 0.0), axis=0, keepdims=True)
        for other in range(4):
            cols = slice(other * 256, other * 256 + 256)
            if (j, other) in where:
                b = where[(j, other)]
                re, im = sg_ref[b, 0], sg_ref[b, 1]
            else:
                b = where[(other, j)]
                re, im = sg_ref[b, 0].T, sg_ref[b, 1].T
            er, ei = rotate(re, im, -ir, -ii)
            for part, value in ((rows, er), (low, ei)):
                if j == other:
                    value = jnp.where(eye, 0.0, value)
                high, rest = split(value)
                shl_ref[0, part, cols] = high
                shl_ref[1, part, cols] = rest
    times(lhs, shl_ref, u_ref, w_ref[0], w_ref[1], R)
    u_ref[0, 0:64, :] += w_ref[0]
    u_ref[1, 0:64, :] += w_ref[1]
    for j in range(4):
        at = pl.multiple_of(j * 256 + g * 16, 16)
        low = pl.multiple_of(j * 256 + g * 16 + R, 16)
        on = lax.broadcasted_iota(jnp.int32, (16, R), 1) == lax.broadcasted_iota(jnp.int32, (16, R), 0) + at
        rows = slice(64 + j * 16, 80 + j * 16)
        er = shl_ref[0, pl.ds(at, 16), :].astype(F32) + shl_ref[1, pl.ds(at, 16), :].astype(F32)
        ei = shl_ref[0, pl.ds(low, 16), :].astype(F32) + shl_ref[1, pl.ds(low, 16), :].astype(F32)
        u_ref[0, rows, :] = jnp.where(on, 1.0, er)
        u_ref[1, rows, :] = ei
    times(lhs, shl_ref, t_ref, u_ref[0], u_ref[1], R)
    times(lhs, shl_ref, t_ref, t_ref[0], t_ref[1], R)
    yr, yi = rotate(u_ref[0] + t_ref[0], u_ref[1] + t_ref[1], d0_ref[0:1, :], d0_ref[1:2, :])
    gw_ref[...] = wr * yr[64:128] - wi * yi[64:128]
    yr, yi = yr[0:64], yi[0:64]
    side = -(wr * yr - wi * yi) * mf_ref[...]
    fw_ref[...] = side
    ft_ref[...] = side.T
    rh, rl = split(yr)
    ih, il = split(yi)
    for at, (re, im) in enumerate(((rh, ih), (rl, il))):
        lhs[at * 128 : at * 128 + 64, 0:R] = re
        lhs[at * 128 + 64 : at * 128 + 128, 0:R] = im
        lhs[at * 128 : at * 128 + 64, R : 2 * R] = -im
        lhs[at * 128 + 64 : at * 128 + 128, R : 2 * R] = re
    wide = dot(lhs[0:256, 0:R], bhl_ref[0, :, 0:C]) + dot(lhs[0:256, R : 2 * R], bhl_ref[0, :, C : 2 * C])
    narrow = dot(lhs[0:128, 0:R], bhl_ref[1, :, 0:C]) + dot(lhs[0:128, R : 2 * R], bhl_ref[1, :, C : 2 * C])
    pr, pi = fold(wide, narrow, 64)
    times(lhs, ehl_ref, k_ref, pr, pi, C)
    ku_ref[0] = k_ref[0] + pr
    ku_ref[1] = k_ref[1] + pi
    times(lhs, ehl_ref, k_ref, ku_ref[0], ku_ref[1], C)
    times(lhs, ehl_ref, k_ref, k_ref[0], k_ref[1], C)
    zr, zi = rotate(ku_ref[0] + k_ref[0], ku_ref[1] + k_ref[1], dinv_ref[0:1, :], dinv_ref[1:2, :])
    dw_ref[...] = wr * (xc_ref[0] + zr) - wi * (xc_ref[1] + zi)


def root_part(scalars, ids, sg, ehl, dinv, bhl, w, xc, mask_f):
    return pl.pallas_call(
        root_kernel,
        name="root_part",
        out_shape=(
            jax.ShapeDtypeStruct((64, C), F32),
            jax.ShapeDtypeStruct((64, R), F32),
            jax.ShapeDtypeStruct((R, 64), F32),
            jax.ShapeDtypeStruct((64, R), F32),
        ),
        in_specs=[SM, SM] + [VM] * 7,
        out_specs=(VM,) * 4,
        scratch_shapes=[
            pltpu.VMEM((2, 2 * R, R), BF16), pltpu.VMEM((8, R), F32), pltpu.VMEM((512, 2 * R), BF16),
            pltpu.VMEM((2, 128, R), F32), pltpu.VMEM((2, 128, R), F32),
            pltpu.VMEM((2, 64, C), F32), pltpu.VMEM((2, 64, C), F32),
        ],
        compiler_params=pltpu.CompilerParams(vmem_limit_bytes=52 << 20),
        cost_estimate=pl.CostEstimate(flops=8 << 30, bytes_accessed=16 << 20, transcendentals=0),
    )(scalars, ids, sg, ehl, dinv, bhl, w, xc, mask_f)


def sum_kernel(
    dw_ref, fw_ref, ft_ref, gw_ref, main_ref, d_ref, e_ref,
    rf_ref, rd_ref, re_ref, ea_ref,
    loc_sem, a_s, a_r, f_s, f_r, d_s, d_r, g_s, e_s, e_r,
):
    p, g, x, yl, z, yh, q, c = place()
    poles = [lax.rem(p + d, 8) for d in range(8)]
    sib = g + 1 - 2 * c
    grids = [lax.rem(g + d, 16) for d in range(1, 16)]
    greet([(pp, g) for pp in poles[1:]] + [(pp, sib) for pp in poles[1:]] + [(p, gg) for gg in grids])
    top = p >= 4
    pending = []

    def go(copy):
        copy.start()
        pending.append(copy)

    for d, gg in enumerate(grids):
        go(remote(ft_ref.at[:, gg], ea_ref.at[g], a_s.at[d], a_r.at[d], (p, gg)))
    keep = pltpu.make_async_copy(ft_ref.at[:, g], ea_ref.at[g], loc_sem.at[0])
    keep.start()
    later = []
    for j in range(4):
        src = gw_ref.at[pl.ds(j * 16, 16), :]
        away = remote(src, rf_ref.at[p], g_s.at[j], f_r.at[p], (4 + j, g))
        stay = pltpu.make_async_copy(src, rf_ref.at[p], g_s.at[j])
        later.append((p == 4 + j, away, stay))
    for jj in (0, 1):
        for cc in (0, 1):
            rows = pl.ds(jj * 32 + cc * 16, 16)
            target = (2 * c + jj, 2 * q + cc)
            here = jnp.logical_and(p == 2 * c + jj, c == cc)
            for src, dst, ss, rs in ((fw_ref, rf_ref, f_s, f_r), (dw_ref, rd_ref, d_s, d_r)):
                away = remote(src.at[rows, :], dst.at[p], ss.at[jj, cc], rs.at[p], target)
                stay = pltpu.make_async_copy(src.at[rows, :], dst.at[p], ss.at[jj, cc])
                later.append((here, away, stay))
    for here, away, stay in later:

        @pl.when(jnp.logical_not(here))
        def _():
            away.start()

        @pl.when(here)
        def _():
            stay.start()

    keep.wait()
    for d in range(15):
        gg = lax.rem(g + 15 - d, 16)
        remote(ea_ref.at[gg], ea_ref.at[gg], a_s.at[d], a_r.at[d], (p, grids[0])).wait_recv()
    last = []
    for j in range(4):
        src = ea_ref.at[:, j]
        away = remote(src, re_ref.at[p], e_s.at[j], e_r.at[p], (4 + j, g))
        stay = pltpu.make_async_copy(src, re_ref.at[p], e_s.at[j])
        last.append((p == 4 + j, away, stay))
    for here, away, stay in last:

        @pl.when(jnp.logical_not(here))
        def _():
            away.start()

        @pl.when(here)
        def _():
            stay.start()

    for here, away, stay in later + last:

        @pl.when(jnp.logical_not(here))
        def _():
            away.wait_send()

        @pl.when(here)
        def _():
            stay.wait()

    other = (lax.rem(p + 1, 8), g)
    same = jnp.logical_or(top, c == half(p))
    for d in range(8):
        pp = poles[d]

        @pl.when(jnp.logical_or(jnp.logical_not(same), d > 0))
        def _():
            remote(rf_ref.at[pp], rf_ref.at[pp], f_s.at[0, 0], f_r.at[pp], other).wait_recv()

        @pl.when(jnp.logical_and(jnp.logical_not(top), jnp.logical_or(jnp.logical_not(same), d > 0)))
        def _():
            remote(rd_ref.at[pp], rd_ref.at[pp], d_s.at[0, 0], d_r.at[pp], other).wait_recv()

    main = rf_ref[0]
    for n in range(1, 8):
        main = main + rf_ref[n]
    main_ref[...] = main

    @pl.when(top)
    def _():
        for d in range(1, 8):
            pp = poles[d]
            remote(re_ref.at[pp], re_ref.at[pp], e_s.at[0], e_r.at[pp], other).wait_recv()
        total = re_ref[0]
        for n in range(1, 8):
            total = total + re_ref[n]
        e_ref[...] = total
        d_ref[...] = jnp.zeros_like(d_ref)

    @pl.when(jnp.logical_not(top))
    def _():
        total = rd_ref[0]
        for n in range(1, 8):
            total = total + rd_ref[n]
        d_ref[...] = total
        e_ref[...] = jnp.zeros_like(e_ref)

    for copy in pending:
        copy.wait_send()


def sum_poles(dw, fw, ft, gw):
    dma = pltpu.SemaphoreType.DMA
    return pl.pallas_call(
        sum_kernel,
        name="sum_poles",
        out_shape=(
            jax.ShapeDtypeStruct((16, R), F32),
            jax.ShapeDtypeStruct((16, C), F32),
            jax.ShapeDtypeStruct((16, 16, 64), F32),
        ),
        in_specs=[VM] * 4,
        out_specs=(VM,) * 3,
        scratch_shapes=[
            pltpu.VMEM((8, 16, R), F32), pltpu.VMEM((8, 16, C), F32), pltpu.VMEM((8, 16, 16, 64), F32),
            pltpu.VMEM((16, 4, 16, 64), F32),
            dma((1,)), dma((15,)), dma((15,)), dma((2, 2)), dma((8,)), dma((2, 2)), dma((8,)),
            dma((4,)), dma((4,)), dma((8,)),
        ],
        compiler_params=pltpu.CompilerParams(
            collective_id=2, has_side_effects=True, vmem_limit_bytes=40 << 20
        ),
        cost_estimate=pl.CostEstimate(flops=0, bytes_accessed=4 << 20, transcendentals=0),
    )(dw, fw, ft.reshape(4, 16, 16, 64), gw)


def local(hamiltonian, margin, pattern, shift_real, shift_imag, residue):
    p = lax.axis_index("pole")
    g = lax.axis_index("grid")
    q, c = g // 2, g % 2
    scalars = jnp.stack([shift_real[0], shift_imag[0], residue[0, 0], residue[0, 1]])
    ids = jnp.stack([q, g]).astype(jnp.int32)
    own = lax.dynamic_slice_in_dim(pattern.astype(F32), 2 * c, 2, 1)
    mask_b = jnp.repeat(own, 256, axis=1)
    mask_f = jnp.repeat(jnp.repeat(own.T, 32, axis=0), 256, axis=1)
    ab, a0 = gather_inputs(hamiltonian, margin)
    ehl, dinv, bhl, tb, w, xc = child_part(scalars, ids, ab, mask_b)
    sg = share_schur(scalars, tb, a0).reshape(NB, 2, 256, 256)
    dw, fw, ft, gw = root_part(scalars, ids, sg, ehl, dinv, bhl, w, xc, mask_f)
    main, diag, side = sum_poles(dw, fw, ft, gw)
    side = side.reshape(8, 2, 16, 2, 32).transpose(2, 1, 3, 0, 4).reshape(16, R)
    zero = jnp.zeros_like(diag)
    left = jnp.where(
        p < 4,
        jnp.concatenate([jnp.where(p < 2, diag, zero), jnp.where(p < 2, zero, diag)], axis=1),
        side,
    )
    return jnp.concatenate([left, main], axis=1)


def solution(mesh):
    return jax.shard_map(
        local,
        mesh=mesh,
        in_specs=(
            P(("pole", "grid"), None),
            P(("pole", "grid"), None),
            P(),
            P("pole"),
            P("pole"),
            P("pole", None),
        ),
        out_specs=P(("pole", "grid"), None),
        check_vma=False,
    )
```

time: 919 us -> 153 us (0.17); the launches traced: 900 us -> 153 us
  waiting for transfers between devices: 519 us -> 0 us
  local copies, waits for them, and re-layouts: 212 us -> 4.03 us
  Pallas kernels: 0 us -> 145 us
  matrix products: 115 us -> 0 us
  other arithmetic: 26.6 us -> 2.79 us
  between operations: 15.7 us -> 1.42 us
  starting transfers between devices: 12.9 us -> 0 us
    all_gather x12 -> x0, waiting for transfers between devices: 442 us -> none  [the longest x2 90.1 us: newton(): lax.all_gather(real, 'grid', axis=2, tiled=True)]
    pallas_call x0 -> x5, Pallas kernels: none -> 145 us  [the longest x1 54 us: gather_inputs(): pl.pallas_call(gather_kernel, name='gather_inputs', out_shape=(jax.ShapeD...]
    reshape x8 -> x2, local copies, waits for them, and re-layouts: 133 us -> 0.33 us  [local(): side = side.reshape(8, 2, 16, 2, 32).transpose(2, 1, 3, 0, 4).reshape(16, R)]
    dot_general x34 -> x0, matrix products: 115 us -> none  [the longest x8 31.1 us: ceinsum(): mult(left[0], right[1]) + mult(left[1], right[0])]
    psum x1 -> x0, waiting for transfers between devices: 74.2 us -> none  [local(): whole_sum = lax.psum(total, 'pole')]
    gather x8 -> x0, local copies, waits for them, and re-layouts: 46.4 us -> none  [the longest x5 23.4 us: newton(): diag_real = jnp.diagonal(whole[0], axis1=1, axis2=2)]
    sub x10 -> x0, other arithmetic: 16.3 us -> none  [the longest x3 8.69 us: cmul(): left[0] * right[0] - left[1] * right[1]]
    unnamed x64 -> x11, local copies, waits for them, and re-layouts: 14.4 us -> 1.8 us
  transfers between devices with their start and end apart: 15 -> 0, of which waited for: 12 -> 0; matrix products, arithmetic and copies ran while one was open for 24% -> 0% of each run, Pallas kernels for 0% -> 0%
where the time goes in v1:
time: 153 us
  Pallas kernels  145 us (95%)
  local copies, waits for them, and re-layouts  4.03 us (3%)
  other arithmetic  2.79 us (2%)
    pallas_call x1, Pallas kernels, gather_inputs(): pl.pallas_call(gather_kernel, name='gather_inputs', out_shape=(jax.ShapeD...  54 us
    pallas_call x1, Pallas kernels, share_schur(): pl.pallas_call(schur_kernel, name='share_schur', out_shape=jax.ShapeDtype...  33 us
    pallas_call x1, Pallas kernels, sum_poles(): pl.pallas_call(sum_kernel, name='sum_poles', out_shape=(jax.ShapeDtypeStr...  29.6 us
    pallas_call x1, Pallas kernels, root_part(): pl.pallas_call(root_kernel, name='root_part', out_shape=(jax.ShapeDtypeSt...  16.6 us
    pallas_call x1, Pallas kernels, child_part(): pl.pallas_call(child_kernel, name='child_part', out_shape=(jax.ShapeDtype...  11.5 us

profile of v1, /device:TPU:1, one launch (start us, length us, event | category | flops | bytes accessed | tf_op | source)
XLA Modules:
  0.0 153.0 jit_solution(16524885886847792924)
XLA Ops:
  0.0 0.7 convert_element_type.3
  0.7 0.1 constant_dynamic-slice_fusion
  0.8 0.1 broadcast_bitcast_fusion
  0.8 0.1 pad_add_fusion.id_ref
  0.9 1.4 fusion
  3.6 1.3 pad_maximum_fusion.1.sc_ref
  4.9 0.0 copy-start.1
  4.9 54.0 %gather_inputs.1 = (f32[2,1536,512]{2,1,0:T(8,128)}, f32[2,64,1024]{2,1,0:T(8,128)}) custom-call(f32[16,2048]{1,0:T(8,128)} %h_ref.1, f32[16,2048]{1,0:T(8,128)} %s_ref.1), custom_call_target="tpu_custom_call" | custom-call | bytes 16777216 | tf_op jit(solution)/shard_map/gather_inputs/pallas_call | solution.py:258
  58.9 11.5 %child_part.1 = (bf16[2,1024,512]{2,1,0:T(8,128)(2,1)}, f32[8,512]{1,0:T(8,128)S(1)}, bf16[2,1024,1024]{2,1,0:T(8,128)(2,1)}, f32[2,10,2,16,256]{4,3,2,1,0:T(8,1...) custom-call(f32[4]{0:T(128)S(1)} %pad_maximum_fusion.1.sc_ref, s32[2]{0:T(128)S(1)} %pad_add_fusion.id_ref, ...), custom_call_target="tpu_custom_call" | custom-call | flops 4294967296 | bytes 16777216 | tf_op jit(solution)/shard_map/child_part/pallas_call | solution.py:413
  70.4 0.0 copy-done.1
  70.5 0.0 copy-start
  70.5 0.9 copy-done
  71.3 0.0 copy-start.3
  71.3 0.8 copy-done.3
  72.1 0.0 copy-start.2
  72.1 33.0 %share_schur.1 = f32[10,2,16,16,256]{4,3,2,1,0:T(8,128)} custom-call(f32[4]{0:T(128)} %copy-done.1, f32[2,10,2,16,256]{4,3,2,1,0:T(8,128)} %copy-done, f32[2,64,1024]{2,1,0:T(8,128)} %get-tuple-element.22.a0_ref), custom_call_target="tpu_custom_call" | custom-call | bytes 16777216 | tf_op jit(solution)/shard_map/share_schur/pallas_call | solution.py:508
  105.2 0.1 fusion.1
  105.2 0.1 copy.7
  105.3 0.1 broadcast_in_dim.14
  105.5 0.0 copy-done.2
  105.5 16.6 %root_part.1 = (f32[64,512]{1,0:T(8,128)S(1)}, f32[64,1024]{1,0:T(8,128)S(1)}, f32[1024,64]{1,0:T(8,128)S(1)}, f32[64,1024]{1,0:T(8,128)S(1)}) custom-call(f32[4]{0:T(128)S(1)} %copy-done.2, s32[2]{0:T(128)S(1)} %pad_add_fusion.id_ref, f32[10,2,256,256]{3,2,1,0:T(8,128)} %bitcast.20, bf16[2,1024,512]{2,1,0:T(8,128)(2,1)} %get-tuple-element.23.ehl_ref, ...), custom_call_target="tpu_custom_call" | custom-call | flops 8589934592 | bytes 16777216 | tf_op jit(solution)/shard_map/root_part/pallas_call | solution.py:598
  122.2 29.6 %sum_poles.1 = (f32[16,1024]{1,0:T(8,128)S(1)}, f32[16,512]{1,0:T(8,128)S(1)}, f32[16,16,64]{2,1,0:T(8,128)S(1)}) custom-call(f32[64,512]{1,0:T(8,128)S(1)} %get-tuple-element.28.dw_ref, f32[64,1024]{1,0:T(8,128)S(1)} %get-tuple-element.29.fw_ref, f32[4,16,16,64]{3,2,1,0:T(8,128)S(1)} %bitcast.17, f32[64,1024]{1,0:T(8,128)S(1)} %get-tuple-element.31.gw_ref), custom_call_target="tpu_custom_call" | custom-call | bytes 4194304 | tf_op jit(solution)/shard_map/sum_poles/pallas_call | solution.py:738
  151.8 0.2 reshape.26
  152.0 0.2 copy.8
  152.1 0.1 reshape.27
  152.3 0.7 pad_maximum_fusion
  (5 shorter events, 0.1 us)
Async XLA Ops:
  4.9 65.5 %copy-start.1 = (f32[4]{0:T(128)}, f32[4]{0:T(128)S(1)}, u32[]{:S(2)}) copy-start(f32[4]{0:T(128)S(1)} %pad_maximum_fusion.1.sc_ref) | copy-start | bytes 52
  70.5 0.9 copy-start
  71.3 0.8 copy-start.3
  72.1 33.4 %copy-start.2 = (f32[4]{0:T(128)S(1)}, f32[4]{0:T(128)}, u32[]{:S(2)}) copy-start(f32[4]{0:T(128)} %copy-done.1) | copy-start | bytes 52

commit v2 on v0

v2 whole, which is shorter than its diff:
```python
import jax
import jax.numpy as jnp
from jax import lax
from jax.experimental import pallas as pl
from jax.experimental.pallas import tpu as pltpu
from jax.sharding import PartitionSpec as P

C = 512
R = 1024
F32 = jnp.float32
BF16 = jnp.bfloat16
MESH = pl.DeviceIdType.MESH
VM = pl.BlockSpec(memory_space=pltpu.VMEM)
SM = pl.BlockSpec(memory_space=pltpu.SMEM)
BLOCKS = ((0, 0), (3, 0), (0, 1), (1, 1), (0, 2), (1, 2), (2, 2), (1, 3), (2, 3), (3, 3))
WHERE = {pair: b for b, pair in enumerate(BLOCKS)}
NB = len(BLOCKS)
GROUPS = (slice(0, 4), slice(4, 10))


def mod4(v):
    return lax.rem(v + 4, 4)


def half(v):
    return lax.div(v, 2)


def place():
    p = lax.axis_index("pole")
    g = lax.axis_index("grid")
    x, yl = half(p), lax.rem(p, 2)
    z, q, c = lax.div(g, 4), half(g), lax.rem(g, 2)
    return p, g, x, yl, z, lax.rem(q, 2), q, c


def spot(x, y, z, c):
    return (2 * x + lax.rem(y, 2), 4 * z + 2 * half(y) + c)


def greet(devices):
    barrier = pltpu.get_barrier_semaphore()
    for device in devices:
        pl.semaphore_signal(barrier, inc=1, device_id=device, device_id_type=MESH)
    pl.semaphore_wait(barrier, len(devices))


def remote(src, dst, send, recv, device):
    return pltpu.make_async_remote_copy(
        src_ref=src, dst_ref=dst, send_sem=send, recv_sem=recv, device_id=device, device_id_type=MESH
    )


def split(v):
    high = v.astype(BF16)
    return high, (v - high.astype(F32)).astype(BF16)


def put_pair(lhs_ref, vr, vi):
    m, k = vr.shape
    rh, rl = split(vr)
    ih, il = split(vi)
    for at, (re, im) in enumerate(((rh, ih), (rl, il))):
        base = at * 2 * m
        lhs_ref[base : base + m, 0:k] = re
        lhs_ref[base : base + m, k : 2 * k] = -im
        lhs_ref[base + m : base + 2 * m, 0:k] = im
        lhs_ref[base + m : base + 2 * m, k : 2 * k] = re


def fold(wide, narrow, m):
    total = wide[0 : 2 * m] + wide[2 * m : 4 * m] + narrow
    return total[0:m], total[m : 2 * m]


def dot(a, b):
    return jnp.dot(a, b, preferred_element_type=F32)


def dot_t(a, b):
    return lax.dot_general(a, b, (((1,), (1,)), ((), ())), preferred_element_type=F32)


def times(lhs_ref, rhs_ref, out_ref, vr, vi, width):
    m, k = vr.shape
    put_pair(lhs_ref, vr, vi)
    for n in range(width // 256):
        cols = slice(n * 256, n * 256 + 256)
        wide = dot(lhs_ref[0 : 4 * m, 0 : 2 * k], rhs_ref[0, :, cols])
        narrow = dot(lhs_ref[0 : 2 * m, 0 : 2 * k], rhs_ref[1, :, cols])
        re, im = fold(wide, narrow, m)
        out_ref[0, 0:m, cols] = re
        out_ref[1, 0:m, cols] = im


def rotate(vr, vi, dr, di):
    return vr * dr - vi * di, vr * di + vi * dr


def recip(dr, di):
    den = dr * dr + di * di
    return dr / den, -di / den


def iota(shape, dim):
    return lax.broadcasted_iota(jnp.int32, shape, dim)


def kernel(
    h_ref, s_ref, pat_ref, sr_ref, si_ref, res_ref, out_ref,
    ab_ref, a0_ref, ehl_ref, bhl_ref, dinv_ref, lhs, cu_ref, ct_ref, xc_ref, w_ref, tb_ref,
    tin_ref, own_ref, sg_ref, shl_ref, d0_ref, u_ref, t_ref,
    k_ref, ku_ref, fw_ref, ft_ref, gw_ref, dw_ref, rf_ref, rd_ref, re_ref, ea_ref,
    loc_sem, sib_s, sib_r, x_s, x_r, f_s, f_r, fo_s, fo_r, g_s, g_r, go_s, go_r,
    y0_s, y0_r, x0_s, x0_r,
    tt_s, tt_r, own_sem, y_s, y_r, yo_s, yo_r, z_s, z_r, o_s, o_r, b_s, b_r,
    keep_sem, a_s, a_r, sf_s, sf_r, sd_s, sd_r, sg_s, se_s, se_r,
):
    p, g, x, yl, z, yh, q, c = place()
    y = 2 * yh + yl
    sr, si = sr_ref[0], si_ref[0]
    wr, wi = res_ref[0, 0], res_ref[0, 1]
    sib = g + 1 - 2 * c
    sibling = (p, sib)
    partner = (p + 1 - 2 * yl, g)
    over = (p, g + 2 - 4 * yh)
    xs = [spot(mod4(x + d), y, z, c) for d in (1, 2, 3)]
    ys = [spot(x, mod4(y + d), z, c) for d in (1, -1)]
    zs = [spot(x, y, mod4(z + d), c) for d in (1, -1)]
    poles = [lax.rem(p + d, 8) for d in range(8)]
    grids = [lax.rem(g + d, 16) for d in range(1, 16)]
    beyond = (partner[0], over[1])
    greet(
        [(pp, g) for pp in poles[1:]] + [(pp, sib) for pp in poles[1:]] + [(p, gg) for gg in grids] + [beyond]
    )

    pending = []

    def go(copy):
        copy.start()
        pending.append(copy)

    first = c == 0

    def pick(a, b):
        return tuple(jnp.where(first, u, v) for u, v in zip(a, b))

    fs = [pick(ys[i], zs[i]) for i in (0, 1)]
    gs = [pick(zs[i], ys[i]) for i in (0, 1)]
    f0 = jnp.where(first, y, z)
    g0 = jnp.where(first, z, y)

    def row(slot, f, s):
        yy, zz = jnp.where(first, f, s), jnp.where(first, s, f)
        return pl.multiple_of(slot * 512 + lax.rem(yy, 2) * 256 + (2 * zz + half(yy)) * 32, 32)

    def slab(slot, f, s):
        return ab_ref.at[:, pl.ds(row(slot, f, s), 32), :]

    def part(slot, f, s, k):
        return ab_ref.at[k, pl.ds(row(slot, f, s), 32), :]

    root = x >= 2
    mine = jnp.logical_or(root, x == c)
    his = jnp.logical_or(root, x == 1 - c)
    slot0 = jnp.maximum(x - 1, 0)
    row0 = pl.multiple_of(slot0 * 512 + yl * 256 + q * 32 + c * 16, 16)
    inputs = (h_ref, s_ref)
    own_cols = pl.ds(pl.multiple_of(c * 512, 128), 512)
    sib_cols = pl.ds(pl.multiple_of((1 - c) * 512, 128), 512)
    dst_rows = pl.ds(row0, 16)
    sib_rows = pl.ds(pl.multiple_of(row0 + (1 - 2 * c) * 16, 16), 16)
    own = [pltpu.make_async_copy(inputs[k].at[:, own_cols], ab_ref.at[k, dst_rows, :], loc_sem.at[k]) for k in (0, 1)]
    to_sib = [
        remote(inputs[k].at[:, sib_cols], ab_ref.at[k, dst_rows, :], sib_s.at[k], sib_r.at[k], sibling)
        for k in (0, 1)
    ]
    from_sib = [
        remote(inputs[k].at[:, own_cols], ab_ref.at[k, sib_rows, :], sib_s.at[k], sib_r.at[k], sibling)
        for k in (0, 1)
    ]
    sx = jnp.maximum(x - 2, 0)
    j0 = 2 * sx + yl
    j1 = 2 * sx + 1 - yl

    def top(k, j):
        return a0_ref.at[k, pl.ds(pl.multiple_of(j * 16, 16), 16), :]

    top_src = [inputs[k].at[:, pl.ds(1024, 1024)] for k in (0, 1)]
    top_own = [pltpu.make_async_copy(top_src[k], top(k, j0), loc_sem.at[2 + k]) for k in (0, 1)]
    top_y = [remote(top_src[k], top(k, j0), y0_s.at[k], y0_r.at[k], partner) for k in (0, 1)]
    top_y_in = [remote(top_src[k], top(k, j1), y0_s.at[k], y0_r.at[k], partner) for k in (0, 1)]
    top_x = [
        remote(top_src[k], top(k, j0), x0_s.at[n, 0, k], x0_r.at[sx, 0, k], xs[n]) for n in range(3) for k in (0, 1)
    ]
    top_x2 = [
        remote(top(k, j1), top(k, j1), x0_s.at[n, 1, k], x0_r.at[sx, 1, k], xs[n]) for n in range(3) for k in (0, 1)
    ]

    @pl.when(his)
    def _():
        for copy in to_sib:
            copy.start()

    @pl.when(mine)
    def _():
        for copy in own:
            copy.start()
        for copy in own:
            copy.wait()
        for copy in from_sib:
            copy.wait_recv()

    to_x = [remote(slab(slot0, f0, g0), slab(slot0, f0, g0), x_s.at[n], x_r.at[slot0], xs[n]) for n in range(3)]

    @pl.when(mine)
    def _():
        for copy in to_x:
            copy.start()

    for slot in range(3):
        not_mine = jnp.logical_or(jnp.logical_not(mine), slot0 != slot)

        @pl.when(not_mine)
        def _():
            remote(slab(slot, f0, g0), slab(slot, f0, g0), x_s.at[0], x_r.at[slot], xs[0]).wait_recv()

    f_at = (f0, mod4(f0 - 1), mod4(f0 + 1), mod4(f0 + 2))
    g_at = (mod4(g0 - 1), mod4(g0 + 1), mod4(g0 + 2))

    def spread(slot, n):
        ref = slab(slot, f_at[n], g0)
        for d in (0, 1):
            go(remote(ref, ref, g_s.at[d, slot, n], g_r.at[d, slot, n], gs[d]))

    def open_slot(slot):
        ref = slab(slot, f0, g0)
        for d in (0, 1):
            go(remote(ref, ref, f_s.at[d, slot], f_r.at[d, slot], fs[d]))
        spread(slot, 0)

    def near(slot):
        for d in (0, 1):
            ref = slab(slot, f_at[1 + d], g0)
            remote(ref, ref, f_s.at[d, slot], f_r.at[d, slot], fs[d]).wait_recv()
            ref = part(slot, f_at[1 + d], g0, d)
            go(remote(ref, ref, fo_s.at[slot, d], fo_r.at[slot, d], fs[d]))
            spread(slot, 1 + d)

    def far(slot):
        for d in (0, 1):
            ref = part(slot, f_at[3], g0, d)
            remote(ref, ref, fo_s.at[slot, d], fo_r.at[slot, d], fs[d]).wait_recv()
        spread(slot, 3)

    def relay(slot, n):
        for d in (0, 1):
            ref = slab(slot, f_at[n], g_at[d])
            remote(ref, ref, g_s.at[d, slot, n], g_r.at[d, slot, n], gs[d]).wait_recv()
            ref = part(slot, f_at[n], g_at[d], d)
            go(remote(ref, ref, go_s.at[slot, n, d], go_r.at[slot, n, d], gs[d]))

    def close_slot(slot):
        for n in range(4):
            for d in (0, 1):
                ref = part(slot, f_at[n], g_at[2], d)
                remote(ref, ref, go_s.at[slot, n, d], go_r.at[slot, n, d], gs[d]).wait_recv()

    def top_start():
        @pl.when(root)
        def _():
            for copy in top_y + top_own + top_x:
                copy.start()

    def top_more():
        @pl.when(root)
        def _():
            for k in (0, 1):
                top_y_in[k].wait_recv()
            for copy in top_x2:
                copy.start()

    dinv_ref[...] = jnp.zeros_like(dinv_ref)

    def scale_rows(n):
        rows = slice(n * 64, n * 64 + 64)
        low = slice(n * 64 + C, n * 64 + C + 64)
        s = ab_ref[1, rows, :]
        re = ab_ref[0, rows, :] - sr * s
        im = -si * s
        eye = iota((64, C), 1) == iota((64, C), 0) + n * 64
        ir, ii = recip(
            jnp.sum(jnp.where(eye, re, 0.0), axis=1, keepdims=True),
            jnp.sum(jnp.where(eye, im, 0.0), axis=1, keepdims=True),
        )
        dinv_ref[0:1, :] += jnp.sum(jnp.where(eye, ir, 0.0), axis=0, keepdims=True)
        dinv_ref[1:2, :] += jnp.sum(jnp.where(eye, ii, 0.0), axis=0, keepdims=True)
        er, ei = rotate(re, im, -ir, -ii)
        for where, value in ((rows, er), (low, ei)):
            high, rest = split(jnp.where(eye, 0.0, value))
            ehl_ref[0, where, :] = high
            ehl_ref[1, where, :] = rest

    def pattern_at(j, half_at):
        return jnp.where(first, pat_ref[j, half_at], pat_ref[j, 2 + half_at]).astype(F32)

    def couple(rows, j):
        m = jnp.where(iota((1, C), 1) < 256, pattern_at(j, 0), pattern_at(j, 1))
        s = ab_ref[1, rows, :] * m
        return ab_ref[0, rows, :] * m - sr * s, -si * s

    def split_rows(n):
        re, im = couple(slice(C + n * 64, C + n * 64 + 64), n // 4)
        rows = slice(n * 64, n * 64 + 64)
        for at, value in ((0, re), (C, im)):
            high, rest = split(value)
            bhl_ref[0, rows, at : at + C] = high
            bhl_ref[1, rows, at : at + C] = rest

    def chain_start():
        for j in range(4):
            re, im = couple(pl.ds(pl.multiple_of(C + j * 256 + q * 32, 32), 32), j)
            ct_ref[0, j * 32 : j * 32 + 32, :] = re
            ct_ref[1, j * 32 : j * 32 + 32, :] = im
        times(lhs, ehl_ref, cu_ref, ct_ref[0, 0:128, :], ct_ref[1, 0:128, :], C)
        cu_ref[0, 0:128, :] += ct_ref[0, 0:128, :]
        cu_ref[1, 0:128, :] += ct_ref[1, 0:128, :]
        for jj in range(2):
            at = pl.multiple_of(jj * 256 + q * 32, 32)
            low = pl.multiple_of(jj * 256 + q * 32 + C, 32)
            eye = iota((32, C), 1) == iota((32, C), 0) + at
            rows = slice(128 + jj * 32, 160 + jj * 32)
            er = ehl_ref[0, pl.ds(at, 32), :].astype(F32) + ehl_ref[1, pl.ds(at, 32), :].astype(F32)
            ei = ehl_ref[0, pl.ds(low, 32), :].astype(F32) + ehl_ref[1, pl.ds(low, 32), :].astype(F32)
            cu_ref[0, rows, :] = jnp.where(eye, 1.0, er)
            cu_ref[1, rows, :] = ei

    def chain_two():
        times(lhs, ehl_ref, ct_ref, cu_ref[0], cu_ref[1], C)

    def chain_three():
        times(lhs, ehl_ref, ct_ref, ct_ref[0], ct_ref[1], C)
        lr, li = rotate(cu_ref[0] + ct_ref[0], cu_ref[1] + ct_ref[1], dinv_ref[0:1, :], dinv_ref[1:2, :])
        xc_ref[0] = lr[128:192]
        xc_ref[1] = li[128:192]
        put_pair(lhs, lr, li)

    def product(n):
        rows = slice(n * 256, n * 256 + 256)
        wide = dot_t(lhs[0:768, 0 : 2 * C], bhl_ref[0, rows, :])
        narrow = dot_t(lhs[0:384, 0 : 2 * C], bhl_ref[1, rows, :])
        pair = fold(wide, narrow, 192)
        for k in (0, 1):
            w_ref[k, :, rows] = pair[k][128:192]
            for b, (j, other) in enumerate(BLOCKS):
                if other == n:
                    for cc in (0, 1):
                        tb_ref[cc, b, k] = pair[k][j * 32 + cc * 16 : j * 32 + cc * 16 + 16]

    for slot in range(3):
        open_slot(slot)
    near(0)
    relay(0, 0)
    near(1)
    far(0)
    top_start()
    relay(1, 0)
    near(2)
    for n in (1, 2):
        relay(0, n)
    relay(2, 0)
    relay(0, 3)
    far(1)
    relay(1, 1)
    far(2)
    relay(1, 2)
    close_slot(0)
    mixed = [
        lambda: scale_rows(0), lambda: scale_rows(1), lambda: relay(2, 1),
        lambda: scale_rows(2), lambda: scale_rows(3), lambda: relay(2, 2),
        lambda: scale_rows(4), lambda: scale_rows(5), lambda: relay(1, 3),
        lambda: scale_rows(6), lambda: scale_rows(7), lambda: relay(2, 3), top_more,
        chain_start, chain_two, chain_three,
        lambda: close_slot(1),
    ] + [lambda n=n: split_rows(n) for n in range(8)] + [
        lambda: close_slot(2),
    ] + [lambda n=n: split_rows(n) for n in range(8, 16)]
    for step in mixed:
        step()

    for sx_in in (0, 1):
        jx = (2 * sx_in + yl, 2 * sx_in + 1 - yl)

        @pl.when(x != 2 + sx_in)
        def _():
            for o in (0, 1):
                for k in (0, 1):
                    ref = top(k, jx[o])
                    remote(ref, ref, x0_s.at[0, o, k], x0_r.at[sx_in, o, k], xs[0]).wait_recv()

    @pl.when(root)
    def _():
        for copy in top_own:
            copy.wait()

    swaps = [
        remote(tb_ref.at[1 - c, blocks], tin_ref.at[blocks], tt_s.at[n], tt_r.at[n], sibling)
        for n, blocks in enumerate(GROUPS_DS)
    ]
    product(0)
    product(1)
    go(swaps[0])
    product(2)
    product(3)
    go(swaps[1])

    def finish(n):
        for b in range(GROUPS[n].start, GROUPS[n].stop):
            j, other = BLOCKS[b]
            s = a0_ref[1, j * 16 : j * 16 + 16, other * 256 : other * 256 + 256]
            h = a0_ref[0, j * 16 : j * 16 + 16, other * 256 : other * 256 + 256]
            own_ref[b, 0] = h - sr * s - tb_ref[c, b, 0]
            own_ref[b, 1] = -si * s - tb_ref[c, b, 1]
        swaps[n].wait_recv()
        rows = GROUPS[n]
        own_ref[rows] = own_ref[rows] - tin_ref[rows]

    def whole(n, gg):
        return sg_ref.at[GROUPS_DS[n], :, gg]

    def piece(n, gg, k):
        return sg_ref.at[GROUPS_DS[n], k, gg]

    base = (g, g + 2 - 4 * yh)
    hop = [0] + [4 * (mod4(z + d) - z) for d in (-1, 1, 2)]

    def hand(n, m, o, ref_of):
        for k in (0, 1):
            ref = piece(n, base[o] + hop[m], k)
            go(remote(ref_of(k), ref, b_s.at[n, m, o, k], b_r.at[n, m, o, k], sibling))

    def along_z(n, o, src):
        dst = whole(n, base[o])
        for d in (0, 1):
            go(remote(dst if src is None else src, dst, z_s.at[d, n, o], z_r.at[d, n, o], zs[d]))

    keeps = []
    for n in (0, 1):
        finish(n)
        src = own_ref.at[GROUPS_DS[n]]
        along_z(n, 0, src)
        go(remote(src, whole(n, g), y_s.at[n], y_r.at[n], over))
        keep = pltpu.make_async_copy(src, whole(n, g), own_sem.at[n])
        keep.start()
        keeps.append(keep)
        hand(n, 0, 0, lambda k, n=n: own_ref.at[GROUPS_DS[n], k])

    def from_over(n):
        ref = whole(n, base[1])
        remote(ref, ref, y_s.at[n], y_r.at[n], over).wait_recv()
        hand(n, 0, 1, lambda k: piece(n, base[1], k))

    def from_z(n, o):
        for d in (0, 1):
            gg = base[o] + hop[1 + d]
            ref = whole(n, gg)
            remote(ref, ref, z_s.at[d, n, o], z_r.at[d, n, o], zs[d]).wait_recv()
            ref = piece(n, gg, d)
            go(remote(ref, ref, o_s.at[n, o, d], o_r.at[n, o, d], zs[d]))
            if n == 0:
                for k in (0, 1):
                    ref = piece(n, gg, k)
                    go(remote(ref, ref, yo_s.at[1 + d, k], yo_r.at[1 + d, k], over))
            hand(n, 1 + d, o, lambda k, gg=gg: piece(n, gg, k))

    def from_far(n, o):
        gg = base[o] + hop[3]
        for k in (0, 1):
            ref = piece(n, gg, k)
            remote(ref, ref, o_s.at[n, o, k], o_r.at[n, o, k], zs[k]).wait_recv()
            if n == 0:
                go(remote(ref, ref, yo_s.at[3, k], yo_r.at[3, k], over))
            go(remote(ref, ref, b_s.at[n, 3, o, k], b_r.at[n, 3, o, k], sibling))

    def over_far(m):
        gg = base[1] + hop[m]
        for k in (0, 1):
            ref = piece(0, gg, k)
            remote(ref, ref, yo_s.at[m, k], yo_r.at[m, k], over).wait_recv()
            go(remote(ref, ref, b_s.at[0, m, 1, k], b_r.at[0, m, 1, k], sibling))

    from_z(0, 0)
    from_over(1)
    along_z(1, 1, None)
    from_over(0)
    from_far(0, 0)
    from_z(1, 0)
    over_far(1)
    over_far(2)
    from_z(1, 1)
    from_far(1, 0)
    over_far(3)
    from_far(1, 1)
    for n in (0, 1):
        for m in range(4):
            for o in (0, 1):
                gg = base[o] + hop[m] + 1 - 2 * c
                for k in (0, 1):
                    ref = piece(n, gg, k)
                    remote(ref, ref, b_s.at[n, m, o, k], b_r.at[n, m, o, k], sibling).wait_recv()
    for keep in keeps:
        keep.wait()

    def block(b, k):
        return sg_ref[b, k].reshape(256, 256)

    eye = iota((256, 256), 1) == iota((256, 256), 0)
    for j in range(4):
        rows = slice(j * 256, j * 256 + 256)
        low = slice(R + j * 256, R + j * 256 + 256)
        b = WHERE[(j, j)]
        ir, ii = recip(
            jnp.sum(jnp.where(eye, block(b, 0), 0.0), axis=1, keepdims=True),
            jnp.sum(jnp.where(eye, block(b, 1), 0.0), axis=1, keepdims=True),
        )
        d0_ref[0:1, rows] = jnp.sum(jnp.where(eye, ir, 0.0), axis=0, keepdims=True)
        d0_ref[1:2, rows] = jnp.sum(jnp.where(eye, ii, 0.0), axis=0, keepdims=True)
        for other in range(4):
            cols = slice(other * 256, other * 256 + 256)
            if (j, other) in WHERE:
                b = WHERE[(j, other)]
                re, im = block(b, 0), block(b, 1)
            else:
                b = WHERE[(other, j)]
                re, im = block(b, 0).T, block(b, 1).T
            er, ei = rotate(re, im, -ir, -ii)
            for where, value in ((rows, er), (low, ei)):
                if j == other:
                    value = jnp.where(eye, 0.0, value)
                high, rest = split(value)
                shl_ref[0, where, cols] = high
                shl_ref[1, where, cols] = rest
    times(lhs, shl_ref, u_ref, w_ref[0], w_ref[1], R)
    u_ref[0, 0:64, :] += w_ref[0]
    u_ref[1, 0:64, :] += w_ref[1]
    for j in range(4):
        at = pl.multiple_of(j * 256 + g * 16, 16)
        low = pl.multiple_of(j * 256 + g * 16 + R, 16)
        on = iota((16, R), 1) == iota((16, R), 0) + at
        rows = slice(64 + j * 16, 80 + j * 16)
        er = shl_ref[0, pl.ds(at, 16), :].astype(F32) + shl_ref[1, pl.ds(at, 16), :].astype(F32)
        ei = shl_ref[0, pl.ds(low, 16), :].astype(F32) + shl_ref[1, pl.ds(low, 16), :].astype(F32)
        u_ref[0, rows, :] = jnp.where(on, 1.0, er)
        u_ref[1, rows, :] = ei
    times(lhs, shl_ref, t_ref, u_ref[0], u_ref[1], R)
    times(lhs, shl_ref, t_ref, t_ref[0], t_ref[1], R)
    yr, yi = rotate(u_ref[0] + t_ref[0], u_ref[1] + t_ref[1], d0_ref[0:1, :], d0_ref[1:2, :])
    gw_ref[...] = wr * yr[64:128] - wi * yi[64:128]
    yr, yi = yr[0:64], yi[0:64]
    weighted = -(wr * yr - wi * yi)
    for j in range(4):
        cols = slice(j * 256, j * 256 + 256)
        m = jnp.where(iota((64, 1), 0) < 32, pattern_at(j, 0), pattern_at(j, 1))
        side = weighted[:, cols] * m
        fw_ref[:, cols] = side
        ft_ref[j] = side.T.reshape(16, 16, 64)

    for d, gg in enumerate(grids):
        go(remote(ft_ref.at[:, gg], ea_ref.at[g], a_s.at[d], a_r.at[d], (p, gg)))
    keep = pltpu.make_async_copy(ft_ref.at[:, g], ea_ref.at[g], keep_sem)
    keep.start()
    sent = []

    def send_or_keep(src, dst, ss, rs, target, here):
        away = remote(src, dst, ss, rs, target)
        stay = pltpu.make_async_copy(src, dst, ss)

        @pl.when(jnp.logical_not(here))
        def _():
            away.start()

        @pl.when(here)
        def _():
            stay.start()

        sent.append((here, away, stay))

    def child_rows(src, dst, ss, rs):
        for jj in (0, 1):
            for cc in (0, 1):
                here = jnp.logical_and(p == 2 * c + jj, c == cc)
                rows = pl.ds(jj * 32 + cc * 16, 16)
                send_or_keep(src.at[rows, :], dst.at[p], ss.at[jj, cc], rs.at[p], (2 * c + jj, 2 * q + cc), here)

    for j in range(4):
        send_or_keep(gw_ref.at[pl.ds(j * 16, 16), :], rf_ref.at[p], sg_s.at[j], sf_r.at[p], (4 + j, g), p == 4 + j)
    child_rows(fw_ref, rf_ref, sf_s, sf_r)

    rh, rl = split(yr)
    ih, il = split(yi)
    for at, (re, im) in enumerate(((rh, ih), (rl, il))):
        lhs[at * 128 : at * 128 + 64, 0:R] = re
        lhs[at * 128 + 64 : at * 128 + 128, 0:R] = im
        lhs[at * 128 : at * 128 + 64, R : 2 * R] = -im
        lhs[at * 128 + 64 : at * 128 + 128, R : 2 * R] = re
    wide = dot(lhs[0:256, 0:R], bhl_ref[0, :, 0:C]) + dot(lhs[0:256, R : 2 * R], bhl_ref[0, :, C : 2 * C])
    narrow = dot(lhs[0:128, 0:R], bhl_ref[1, :, 0:C]) + dot(lhs[0:128, R : 2 * R], bhl_ref[1, :, C : 2 * C])
    pr, pi = fold(wide, narrow, 64)

    keep.wait()
    for d in range(15):
        gg = lax.rem(g + 15 - d, 16)
        remote(ea_ref.at[gg], ea_ref.at[gg], a_s.at[d], a_r.at[d], (p, grids[0])).wait_recv()
    for j in range(4):
        send_or_keep(ea_ref.at[:, j], re_ref.at[p], se_s.at[j], se_r.at[p], (4 + j, g), p == 4 + j)

    times(lhs, ehl_ref, k_ref, pr, pi, C)
    ku_ref[0] = k_ref[0] + pr
    ku_ref[1] = k_ref[1] + pi
    times(lhs, ehl_ref, k_ref, ku_ref[0], ku_ref[1], C)
    times(lhs, ehl_ref, k_ref, k_ref[0], k_ref[1], C)
    zr, zi = rotate(ku_ref[0] + k_ref[0], ku_ref[1] + k_ref[1], dinv_ref[0:1, :], dinv_ref[1:2, :])
    dw_ref[...] = wr * (xc_ref[0] + zr) - wi * (xc_ref[1] + zi)
    child_rows(dw_ref, rd_ref, sd_s, sd_r)

    for here, away, stay in sent:

        @pl.when(jnp.logical_not(here))
        def _():
            away.wait_send()

        @pl.when(here)
        def _():
            stay.wait()

    lead = p >= 4
    same = jnp.logical_or(lead, c == half(p))
    for d in range(8):
        pp = poles[d]

        @pl.when(jnp.logical_or(jnp.logical_not(same), d > 0))
        def _():
            remote(rf_ref.at[pp], rf_ref.at[pp], sf_s.at[0, 0], sf_r.at[pp], partner).wait_recv()

        @pl.when(jnp.logical_and(jnp.logical_not(lead), jnp.logical_or(jnp.logical_not(same), d > 0)))
        def _():
            remote(rd_ref.at[pp], rd_ref.at[pp], sd_s.at[0, 0], sd_r.at[pp], partner).wait_recv()

    def total(ref):
        value = ref[0]
        for n in range(1, 8):
            value = value + ref[n]
        return value

    out_ref[:, R : 2 * R] = total(rf_ref)

    @pl.when(lead)
    def _():
        for d in range(1, 8):
            pp = poles[d]
            remote(re_ref.at[pp], re_ref.at[pp], se_s.at[0], se_r.at[pp], partner).wait_recv()
        side = total(re_ref)
        for k in (0, 1):
            for jj in (0, 1):
                cols = [side[2 * qq + k][:, jj * 32 : jj * 32 + 32] for qq in range(8)]
                at = k * 512 + jj * 256
                out_ref[:, at : at + 256] = jnp.concatenate(cols, axis=1)

    @pl.when(jnp.logical_not(lead))
    def _():
        diag = total(rd_ref)
        upper = p < 2
        out_ref[:, 0:C] = jnp.where(upper, diag, 0.0)
        out_ref[:, C : 2 * C] = jnp.where(upper, 0.0, diag)

    for copy in pending:
        copy.wait_send()

    @pl.when(his)
    def _():
        for copy in to_sib:
            copy.wait_send()

    @pl.when(mine)
    def _():
        for copy in to_x:
            copy.wait_send()

    @pl.when(root)
    def _():
        for copy in top_y + top_x + top_x2:
            copy.wait_send()


GROUPS_DS = tuple(pl.ds(blocks.start, blocks.stop - blocks.start) for blocks in GROUPS)


def local(hamiltonian, margin, pattern, shift_real, shift_imag, residue):
    dma = pltpu.SemaphoreType.DMA
    vm = pltpu.VMEM
    return pl.pallas_call(
        kernel,
        name="selected_inversion",
        out_shape=jax.ShapeDtypeStruct((16, 2 * R), F32),
        in_specs=[VM, VM, SM, SM, SM, SM],
        out_specs=VM,
        scratch_shapes=[
            vm((2, 1536, 512), F32), vm((2, 64, 1024), F32), vm((2, 1024, C), BF16), vm((2, R, 2 * C), BF16),
            vm((8, C), F32), vm((768, 2 * R), BF16), vm((2, 192, C), F32), vm((2, 192, C), F32),
            vm((2, 64, C), F32), vm((2, 64, R), F32), vm((2, NB, 2, 16, 256), F32),
            vm((NB, 2, 16, 256), F32), vm((NB, 2, 16, 256), F32), vm((NB, 2, 16, 16, 256), F32),
            vm((2, 2 * R, R), BF16), vm((8, R), F32), vm((2, 128, R), F32), vm((2, 128, R), F32),
            vm((2, 64, C), F32), vm((2, 64, C), F32), vm((64, R), F32), vm((4, 16, 16, 64), F32),
            vm((64, R), F32), vm((64, C), F32),
            vm((8, 16, R), F32), vm((8, 16, C), F32), vm((8, 16, 16, 64), F32), vm((16, 4, 16, 64), F32),
            dma((4,)), dma((2,)), dma((2,)), dma((3,)), dma((3,)),
            dma((2, 3)), dma((2, 3)), dma((3, 2)), dma((3, 2)),
            dma((2, 3, 4)), dma((2, 3, 4)), dma((3, 4, 2)), dma((3, 4, 2)),
            dma((2,)), dma((2,)), dma((3, 2, 2)), dma((2, 2, 2)),
            dma((2,)), dma((2,)), dma((2,)), dma((2,)), dma((2,)), dma((4, 2)), dma((4, 2)),
            dma((2, 2, 2)), dma((2, 2, 2)), dma((2, 2, 2)), dma((2, 2, 2)),
            dma((2, 4, 2, 2)), dma((2, 4, 2, 2)),
            dma, dma((15,)), dma((15,)), dma((2, 2)), dma((8,)), dma((2, 2)), dma((8,)),
            dma((4,)), dma((4,)), dma((8,)),
        ],
        compiler_params=pltpu.CompilerParams(
            collective_id=0, has_side_effects=True, vmem_limit_bytes=56 << 20
        ),
        cost_estimate=pl.CostEstimate(flops=12 << 30, bytes_accessed=1 << 20, transcendentals=0),
    )(hamiltonian, margin, pattern, shift_real, shift_imag, residue)


def solution(mesh):
    return jax.shard_map(
        local,
        mesh=mesh,
        in_specs=(
            P(("pole", "grid"), None),
            P(("pole", "grid"), None),
            P(),
            P("pole"),
            P("pole"),
            P("pole", None),
        ),
        out_specs=P(("pole", "grid"), None),
        check_vma=False,
    )
```

time: 919 us -> 122 us (0.13); the launches traced: 900 us -> 122 us
  waiting for transfers between devices: 519 us -> 0 us
  local copies, waits for them, and re-layouts: 212 us -> 1.57 us
  Pallas kernels: 0 us -> 119 us
  matrix products: 115 us -> 0 us
  other arithmetic: 26.6 us -> 0 us
  between operations: 15.7 us -> 1.31 us
  starting transfers between devices: 12.9 us -> 0 us
    all_gather x12 -> x0, waiting for transfers between devices: 442 us -> none  [the longest x2 90.1 us: newton(): lax.all_gather(real, 'grid', axis=2, tiled=True)]
    reshape x8 -> x0, local copies, waits for them, and re-layouts: 133 us -> none  [the longest x1 61.2 us: newton(): whole_imag.reshape(batch, width, width)]
    pallas_call x0 -> x1, Pallas kernels: none -> 119 us  [local(): pl.pallas_call(kernel, name='selected_inversion', out_shape=jax.ShapeDtyp...]
    dot_general x34 -> x0, matrix products: 115 us -> none  [the longest x8 31.1 us: ceinsum(): mult(left[0], right[1]) + mult(left[1], right[0])]
    psum x1 -> x0, waiting for transfers between devices: 74.2 us -> none  [local(): whole_sum = lax.psum(total, 'pole')]
    gather x8 -> x0, local copies, waits for them, and re-layouts: 46.4 us -> none  [the longest x5 23.4 us: newton(): diag_real = jnp.diagonal(whole[0], axis1=1, axis2=2)]
    sub x10 -> x0, other arithmetic: 16.3 us -> none  [the longest x3 8.69 us: cmul(): left[0] * right[0] - left[1] * right[1]]
    unnamed x64 -> x1, local copies, waits for them, and re-layouts: 14.4 us -> 1.57 us
  transfers between devices with their start and end apart: 15 -> 0, of which waited for: 12 -> 0; matrix products, arithmetic and copies ran while one was open for 24% -> 0% of each run, Pallas kernels for 0% -> 0%
where the time goes in v2:
time: 122 us
  Pallas kernels  119 us (98%)
  local copies, waits for them, and re-layouts  1.57 us (1%)
  between operations  1.31 us (1%)
    pallas_call x1, Pallas kernels, local(): pl.pallas_call(kernel, name='selected_inversion', out_shape=jax.ShapeDtyp...  119 us

profile of v2, /device:TPU:1, one launch (start us, length us, event | category | flops | bytes accessed | tf_op | source)
XLA Modules:
  0.0 122.0 jit_solution(2852799818411604897)
XLA Ops:
  1.3 119.1 %selected_inversion.1 = f32[16,2048]{1,0:T(8,128)} custom-call(f32[16,2048]{1,0:T(8,128)} %h_ref.1, f32[16,2048]{1,0:T(8,128)} %s_ref.1, s32[4,4]{1,0:T(4,128)} %pat_ref.1, f32[1]{0:T(128)S(6)} %copy.8.sr_ref, f32[1]{0:T(128)S(6)} %copy.9.si_ref, f32[1,2]{1,0:T(1,128)} %res_ref.1), custom_call_target="tpu_custom_call" | custom-call | flops 12884901888 | bytes 1048576 | tf_op jit(solution)/shard_map/selected_inversion/pallas_call | solution.py:701
  120.4 1.6 %copy.10 = f32[16,2048]{1,0:T(8,128)} copy(f32[16,2048]{1,0:T(8,128)} %selected_inversion.1) | data formatting | bytes 262144

commit v3 on v2

--- a/solution.py
+++ b/solution.py
@@ -108,11 +108,11 @@
 
 def kernel(
     h_ref, s_ref, pat_ref, sr_ref, si_ref, res_ref, out_ref,
-    ab_ref, a0_ref, ehl_ref, bhl_ref, dinv_ref, lhs, cu_ref, ct_ref, xc_ref, w_ref, tb_ref,
+    hs_ref, ab_ref, lb_ref, a0_ref, ehl_ref, bhl_ref, dinv_ref, lhs, cu_ref, ct_ref, xc_ref, w_ref, tb_ref,
     tin_ref, own_ref, sg_ref, shl_ref, d0_ref, u_ref, t_ref,
     k_ref, ku_ref, fw_ref, ft_ref, gw_ref, dw_ref, rf_ref, rd_ref, re_ref, ea_ref,
-    loc_sem, sib_s, sib_r, x_s, x_r, f_s, f_r, fo_s, fo_r, g_s, g_r, go_s, go_r,
-    y0_s, y0_r, x0_s, x0_r,
+    loc_sem, x_s, x_r, f_s, f_r, fo_s, fo_r, g_s, g_r, go_s, go_r,
+    lb_s, lb_r, xl_s, xl_r, xo_s, xo_r, y0_s, y0_r, x0_s, x0_r,
     tt_s, tt_r, own_sem, y_s, y_r, yo_s, yo_r, z_s, z_r, o_s, o_r, b_s, b_r,
     keep_sem, a_s, a_r, sf_s, sf_r, sd_s, sd_r, sg_s, se_s, se_r,
 ):
@@ -130,6 +130,8 @@
     poles = [lax.rem(p + d, 8) for d in range(8)]
     grids = [lax.rem(g + d, 16) for d in range(1, 16)]
     beyond = (partner[0], over[1])
+    hs_ref[0] = h_ref[...]
+    hs_ref[1] = s_ref[...]
     greet(
         [(pp, g) for pp in poles[1:]] + [(pp, sib) for pp in poles[1:]] + [(p, gg) for gg in grids] + [beyond]
     )
@@ -154,31 +156,68 @@
         yy, zz = jnp.where(first, f, s), jnp.where(first, s, f)
         return pl.multiple_of(slot * 512 + lax.rem(yy, 2) * 256 + (2 * zz + half(yy)) * 32, 32)
 
+    def quarter(xx):
+        return pl.ds(pl.multiple_of(xx * 128, 128), 128)
+
     def slab(slot, f, s):
-        return ab_ref.at[:, pl.ds(row(slot, f, s), 32), :]
+        rows = pl.ds(row(slot, f, s), 32)
+        return ab_ref.at[:, rows, :] if slot < 2 else ab_ref.at[:, rows, quarter(x)]
 
     def part(slot, f, s, k):
-        return ab_ref.at[k, pl.ds(row(slot, f, s), 32), :]
+        rows = pl.ds(row(slot, f, s), 32)
+        return ab_ref.at[k, rows, :] if slot < 2 else ab_ref.at[k, rows, quarter(x)]
+
+    def own_slab(slot):
+        return slab(slot, f0, g0) if slot < 2 else lb_ref.at[:, yl, :, quarter(x)]
 
     root = x >= 2
-    mine = jnp.logical_or(root, x == c)
-    his = jnp.logical_or(root, x == 1 - c)
-    slot0 = jnp.maximum(x - 1, 0)
-    row0 = pl.multiple_of(slot0 * 512 + yl * 256 + q * 32 + c * 16, 16)
-    inputs = (h_ref, s_ref)
-    own_cols = pl.ds(pl.multiple_of(c * 512, 128), 512)
-    sib_cols = pl.ds(pl.multiple_of((1 - c) * 512, 128), 512)
-    dst_rows = pl.ds(row0, 16)
-    sib_rows = pl.ds(pl.multiple_of(row0 + (1 - 2 * c) * 16, 16), 16)
-    own = [pltpu.make_async_copy(inputs[k].at[:, own_cols], ab_ref.at[k, dst_rows, :], loc_sem.at[k]) for k in (0, 1)]
-    to_sib = [
-        remote(inputs[k].at[:, sib_cols], ab_ref.at[k, dst_rows, :], sib_s.at[k], sib_r.at[k], sibling)
-        for k in (0, 1)
-    ]
-    from_sib = [
-        remote(inputs[k].at[:, own_cols], ab_ref.at[k, sib_rows, :], sib_s.at[k], sib_r.at[k], sibling)
-        for k in (0, 1)
-    ]
+    peers = [[spot(mod4(x + d), y, z, cc) for cc in (c, 1 - c)] for d in range(4)]
+
+    def land(slot, cc):
+        if slot == 2:
+            return lb_ref.at[:, yl, pl.ds(pl.multiple_of(cc * 16, 16), 16), :]
+        return ab_ref.at[:, pl.ds(pl.multiple_of(slot * 512 + yl * 256 + q * 32 + cc * 16, 16), 16), :]
+
+    def child_cols(k):
+        return hs_ref.at[:, :, pl.ds(pl.multiple_of(k * 512, 128), 512)]
+
+    def stay_put(slot):
+        return pltpu.make_async_copy(child_cols(c), land(slot, c), loc_sem.at[slot])
+
+    def give(slot, d, e):
+        return remote(
+            child_cols(c if e == 0 else 1 - c), land(slot, c), x_s.at[d, e], x_r.at[slot, e], peers[d][e]
+        )
+
+    def givers(slot):
+        if slot > 0:
+            away = [give(slot, d, e) for d in range(4) for e in (0, 1) if d + e > 0]
+            return [(x == slot + 1, [stay_put(slot)], away)]
+        return [
+            (jnp.logical_and(x < 2, x == c), [stay_put(0)], [give(0, d, 0) for d in (1, 2, 3)]),
+            (jnp.logical_and(x < 2, x != c), [], [give(0, d, 1) for d in range(4)]),
+        ]
+
+    gifts = givers(2) + givers(0) + givers(1)
+    for when, here, away in gifts:
+
+        @pl.when(when)
+        def _():
+            for copy in away + here:
+                copy.start()
+
+    def taken(slot):
+        source = c if slot == 0 else slot + 1
+        remote(land(slot, 1 - c), land(slot, 1 - c), x_s.at[1, 1], x_r.at[slot, 1], peers[1][1]).wait_recv()
+
+        @pl.when(x != source)
+        def _():
+            remote(land(slot, c), land(slot, c), x_s.at[1, 0], x_r.at[slot, 0], peers[1][0]).wait_recv()
+
+        @pl.when(x == source)
+        def _():
+            stay_put(slot).wait()
+
     sx = jnp.maximum(x - 2, 0)
     j0 = 2 * sx + yl
     j1 = 2 * sx + 1 - yl
@@ -186,8 +225,8 @@
     def top(k, j):
         return a0_ref.at[k, pl.ds(pl.multiple_of(j * 16, 16), 16), :]
 
-    top_src = [inputs[k].at[:, pl.ds(1024, 1024)] for k in (0, 1)]
-    top_own = [pltpu.make_async_copy(top_src[k], top(k, j0), loc_sem.at[2 + k]) for k in (0, 1)]
+    top_src = [hs_ref.at[k, :, pl.ds(1024, 1024)] for k in (0, 1)]
+    top_own = [pltpu.make_async_copy(top_src[k], top(k, j0), loc_sem.at[3 + k]) for k in (0, 1)]
     top_y = [remote(top_src[k], top(k, j0), y0_s.at[k], y0_r.at[k], partner) for k in (0, 1)]
     top_y_in = [remote(top_src[k], top(k, j1), y0_s.at[k], y0_r.at[k], partner) for k in (0, 1)]
     top_x = [
@@ -197,46 +236,19 @@
         remote(top(k, j1), top(k, j1), x0_s.at[n, 1, k], x0_r.at[sx, 1, k], xs[n]) for n in range(3) for k in (0, 1)
     ]
 
-    @pl.when(his)
-    def _():
-        for copy in to_sib:
-            copy.start()
-
-    @pl.when(mine)
-    def _():
-        for copy in own:
-            copy.start()
-        for copy in own:
-            copy.wait()
-        for copy in from_sib:
-            copy.wait_recv()
-
-    to_x = [remote(slab(slot0, f0, g0), slab(slot0, f0, g0), x_s.at[n], x_r.at[slot0], xs[n]) for n in range(3)]
-
-    @pl.when(mine)
-    def _():
-        for copy in to_x:
-            copy.start()
-
-    for slot in range(3):
-        not_mine = jnp.logical_or(jnp.logical_not(mine), slot0 != slot)
-
-        @pl.when(not_mine)
-        def _():
-            remote(slab(slot, f0, g0), slab(slot, f0, g0), x_s.at[0], x_r.at[slot], xs[0]).wait_recv()
-
     f_at = (f0, mod4(f0 - 1), mod4(f0 + 1), mod4(f0 + 2))
     g_at = (mod4(g0 - 1), mod4(g0 + 1), mod4(g0 + 2))
 
     def spread(slot, n):
-        ref = slab(slot, f_at[n], g0)
-        for d in (0, 1):
-            go(remote(ref, ref, g_s.at[d, slot, n], g_r.at[d, slot, n], gs[d]))
+        dst = slab(slot, f_at[n], g0)
+        ref = own_slab(slot) if n == 0 else dst
+        for d in (0, 1):
+            go(remote(ref, dst, g_s.at[d, slot, n], g_r.at[d, slot, n], gs[d]))
 
     def open_slot(slot):
-        ref = slab(slot, f0, g0)
-        for d in (0, 1):
-            go(remote(ref, ref, f_s.at[d, slot], f_r.at[d, slot], fs[d]))
+        taken(slot)
+        for d in (0, 1):
+            go(remote(own_slab(slot), slab(slot, f0, g0), f_s.at[d, slot], f_r.at[d, slot], fs[d]))
         spread(slot, 0)
 
     def near(slot):
@@ -265,6 +277,41 @@
             for d in (0, 1):
                 ref = part(slot, f_at[n], g_at[2], d)
                 remote(ref, ref, go_s.at[slot, n, d], go_r.at[slot, n, d], gs[d]).wait_recv()
+
+    def last_rows():
+        ref = lb_ref.at[:, yl]
+        go(remote(ref, ref, lb_s, lb_r, partner))
+        pltpu.make_async_copy(own_slab(2), slab(2, f0, g0), loc_sem.at[5]).start()
+
+    def last_rows_in():
+        ref = lb_ref.at[:, 1 - yl]
+        remote(ref, ref, lb_s, lb_r, partner).wait_recv()
+
+    xx_at = (mod4(x - 1), mod4(x + 1), mod4(x + 2))
+    along = (peers[1][0], peers[3][0])
+
+    def column(xx):
+        return ab_ref.at[:, pl.ds(1024, 512), quarter(xx)]
+
+    def column_part(xx, k):
+        return ab_ref.at[k, pl.ds(1024, 512), quarter(xx)]
+
+    def join():
+        pltpu.make_async_copy(own_slab(2), slab(2, f0, g0), loc_sem.at[5]).wait()
+        for d in (0, 1):
+            go(remote(column(x), column(x), xl_s.at[d], xl_r.at[d], along[d]))
+
+    def join_more():
+        for d in (0, 1):
+            ref = column(xx_at[d])
+            remote(ref, ref, xl_s.at[d], xl_r.at[d], along[d]).wait_recv()
+            ref = column_part(xx_at[d], d)
+            go(remote(ref, ref, xo_s.at[d], xo_r.at[d], along[d]))
+
+    def join_end():
+        for d in (0, 1):
+            ref = column_part(xx_at[2], d)
+            remote(ref, ref, xo_s.at[d], xo_r.at[d], along[d]).wait_recv()
 
     def top_start():
         @pl.when(root)
@@ -304,13 +351,14 @@
     def pattern_at(j, half_at):
         return jnp.where(first, pat_ref[j, half_at], pat_ref[j, 2 + half_at]).astype(F32)
 
-    def couple(rows, j):
+    def couple(h, s, j):
         m = jnp.where(iota((1, C), 1) < 256, pattern_at(j, 0), pattern_at(j, 1))
-        s = ab_ref[1, rows, :] * m
-        return ab_ref[0, rows, :] * m - sr * s, -si * s
+        s = s * m
+        return h * m - sr * s, -si * s
 
     def split_rows(n):
-        re, im = couple(slice(C + n * 64, C + n * 64 + 64), n // 4)
+        rows = slice(C + n * 64, C + n * 64 + 64)
+        re, im = couple(ab_ref[0, rows, :], ab_ref[1, rows, :], n // 4)
         rows = slice(n * 64, n * 64 + 64)
         for at, value in ((0, re), (C, im)):
             high, rest = split(value)
@@ -319,7 +367,11 @@
 
     def chain_start():
         for j in range(4):
-            re, im = couple(pl.ds(pl.multiple_of(C + j * 256 + q * 32, 32), 32), j)
+            if j < 2:
+                rows = pl.ds(pl.multiple_of(C + j * 256 + q * 32, 32), 32)
+                re, im = couple(ab_ref[0, rows, :], ab_ref[1, rows, :], j)
+            else:
+                re, im = couple(lb_ref[0, j - 2], lb_ref[1, j - 2], j)
             ct_ref[0, j * 32 : j * 32 + 32, :] = re
             ct_ref[1, j * 32 : j * 32 + 32, :] = im
         times(lhs, ehl_ref, cu_ref, ct_ref[0, 0:128, :], ct_ref[1, 0:128, :], C)
@@ -357,35 +409,21 @@
                     for cc in (0, 1):
                         tb_ref[cc, b, k] = pair[k][j * 32 + cc * 16 : j * 32 + cc * 16 + 16]
 
-    for slot in range(3):
-        open_slot(slot)
-    near(0)
-    relay(0, 0)
-    near(1)
-    far(0)
-    top_start()
-    relay(1, 0)
-    near(2)
-    for n in (1, 2):
-        relay(0, n)
-    relay(2, 0)
-    relay(0, 3)
-    far(1)
-    relay(1, 1)
-    far(2)
-    relay(1, 2)
-    close_slot(0)
-    mixed = [
-        lambda: scale_rows(0), lambda: scale_rows(1), lambda: relay(2, 1),
-        lambda: scale_rows(2), lambda: scale_rows(3), lambda: relay(2, 2),
-        lambda: scale_rows(4), lambda: scale_rows(5), lambda: relay(1, 3),
-        lambda: scale_rows(6), lambda: scale_rows(7), lambda: relay(2, 3), top_more,
-        chain_start, chain_two, chain_three,
-        lambda: close_slot(1),
+    steps = [
+        lambda: open_slot(2), last_rows, lambda: open_slot(0), lambda: open_slot(1), top_start,
+        lambda: near(2), lambda: relay(2, 0), lambda: near(0), lambda: far(2),
+        lambda: relay(2, 1), lambda: relay(2, 2), lambda: near(1), lambda: relay(0, 0),
+        lambda: relay(2, 3), lambda: far(0), lambda: close_slot(2), join, top_more,
+        lambda: relay(1, 0), lambda: relay(0, 1), lambda: relay(0, 2), lambda: far(1),
+        lambda: relay(0, 3), lambda: relay(1, 1), last_rows_in, lambda: close_slot(0),
+        lambda: scale_rows(0), lambda: scale_rows(1), lambda: relay(1, 2),
+        lambda: scale_rows(2), lambda: scale_rows(3), lambda: scale_rows(4), join_more,
+        lambda: scale_rows(5), lambda: scale_rows(6), lambda: scale_rows(7), lambda: relay(1, 3),
+        chain_start, chain_two, chain_three, lambda: close_slot(1),
     ] + [lambda n=n: split_rows(n) for n in range(8)] + [
-        lambda: close_slot(2),
+        lambda: product(0), lambda: product(1), join_end,
     ] + [lambda n=n: split_rows(n) for n in range(8, 16)]
-    for step in mixed:
+    for step in steps:
         step()
 
     for sx_in in (0, 1):
@@ -407,8 +445,6 @@
         remote(tb_ref.at[1 - c, blocks], tin_ref.at[blocks], tt_s.at[n], tt_r.at[n], sibling)
         for n, blocks in enumerate(GROUPS_DS)
     ]
-    product(0)
-    product(1)
     go(swaps[0])
     product(2)
     product(3)
@@ -676,15 +712,12 @@
     for copy in pending:
         copy.wait_send()
 
-    @pl.when(his)
-    def _():
-        for copy in to_sib:
-            copy.wait_send()
-
-    @pl.when(mine)
-    def _():
-        for copy in to_x:
-            copy.wait_send()
+    for when, here, away in gifts:
+
+        @pl.when(when)
+        def _():
+            for copy in away:
+                copy.wait_send()
 
     @pl.when(root)
     def _():
@@ -705,7 +738,7 @@
         in_specs=[VM, VM, SM, SM, SM, SM],
         out_specs=VM,
         scratch_shapes=[
-            vm((2, 1536, 512), F32), vm((2, 64, 1024), F32), vm((2, 1024, C), BF16), vm((2, R, 2 * C), BF16),
+            vm((2, 16, 2 * R), F32), vm((2, 1536, 512), F32), vm((2, 2, 32, 512), F32), vm((2, 64, 1024), F32), vm((2, 1024, C), BF16), vm((2, R, 2 * C), BF16),
             vm((8, C), F32), vm((768, 2 * R), BF16), vm((2, 192, C), F32), vm((2, 192, C), F32),
             vm((2, 64, C), F32), vm((2, 64, R), F32), vm((2, NB, 2, 16, 256), F32),
             vm((NB, 2, 16, 256), F32), vm((NB, 2, 16, 256), F32), vm((NB, 2, 16, 16, 256), F32),
@@ -713,9 +746,10 @@
             vm((2, 64, C), F32), vm((2, 64, C), F32), vm((64, R), F32), vm((4, 16, 16, 64), F32),
             vm((64, R), F32), vm((64, C), F32),
             vm((8, 16, R), F32), vm((8, 16, C), F32), vm((8, 16, 16, 64), F32), vm((16, 4, 16, 64), F32),
-            dma((4,)), dma((2,)), dma((2,)), dma((3,)), dma((3,)),
+            dma((6,)), dma((4, 2)), dma((3, 2)),
             dma((2, 3)), dma((2, 3)), dma((3, 2)), dma((3, 2)),
             dma((2, 3, 4)), dma((2, 3, 4)), dma((3, 4, 2)), dma((3, 4, 2)),
+            dma, dma, dma((2,)), dma((2,)), dma((2,)), dma((2,)),
             dma((2,)), dma((2,)), dma((3, 2, 2)), dma((2, 2, 2)),
             dma((2,)), dma((2,)), dma((2,)), dma((2,)), dma((2,)), dma((4, 2)), dma((4, 2)),
             dma((2, 2, 2)), dma((2, 2, 2)), dma((2, 2, 2)), dma((2, 2, 2)),

time: 122 us -> 129 us (1.057)
  Pallas kernels: 119 us -> 126 us
    pallas_call x1, Pallas kernels: 119 us -> 126 us  [local(): pl.pallas_call(kernel, name='selected_inversion', out_shape=jax.ShapeDtyp...]
where the time goes in v3:
time: 129 us
  Pallas kernels  126 us (98%)
  local copies, waits for them, and re-layouts  1.57 us (1%)
  between operations  1.31 us (1%)
    pallas_call x1, Pallas kernels, local(): pl.pallas_call(kernel, name='selected_inversion', out_shape=jax.ShapeDtyp...  126 us

profile of v3, /device:TPU:1, one launch (start us, length us, event | category | flops | bytes accessed | tf_op | source)
XLA Modules:
  0.0 129.2 jit_solution(14635787258599853557)
XLA Ops:
  1.3 126.3 %selected_inversion.1 = f32[16,2048]{1,0:T(8,128)} custom-call(f32[16,2048]{1,0:T(8,128)} %h_ref.1, f32[16,2048]{1,0:T(8,128)} %s_ref.1, s32[4,4]{1,0:T(4,128)} %pat_ref.1, f32[1]{0:T(128)S(6)} %copy.8.sr_ref, f32[1]{0:T(128)S(6)} %copy.9.si_ref, f32[1,2]{1,0:T(1,128)} %res_ref.1), custom_call_target="tpu_custom_call" | custom-call | flops 12884901888 | bytes 1048576 | tf_op jit(solution)/shard_map/selected_inversion/pallas_call | solution.py:734
  127.6 1.6 %copy.10 = f32[16,2048]{1,0:T(8,128)} copy(f32[16,2048]{1,0:T(8,128)} %selected_inversion.1) | data formatting | bytes 262144

commit v4 on v3

--- a/solution.py
+++ b/solution.py
@@ -56,12 +56,12 @@
     return high, (v - high.astype(F32)).astype(BF16)
 
 
-def put_pair(lhs_ref, vr, vi):
+def put_pair(lhs_ref, vr, vi, start=0):
     m, k = vr.shape
     rh, rl = split(vr)
     ih, il = split(vi)
     for at, (re, im) in enumerate(((rh, ih), (rl, il))):
-        base = at * 2 * m
+        base = start + at * 2 * m
         lhs_ref[base : base + m, 0:k] = re
         lhs_ref[base : base + m, k : 2 * k] = -im
         lhs_ref[base + m : base + 2 * m, 0:k] = im
@@ -107,12 +107,12 @@
 
 
 def kernel(
-    h_ref, s_ref, pat_ref, sr_ref, si_ref, res_ref, out_ref,
-    hs_ref, ab_ref, lb_ref, a0_ref, ehl_ref, bhl_ref, dinv_ref, lhs, cu_ref, ct_ref, xc_ref, w_ref, tb_ref,
+    h_ref, s_ref, pat_ref, sr_ref, si_ref, res_ref, left_ref, right_ref,
+    hs_ref, ab_ref, a0_ref, ehl_ref, bhl_ref, dinv_ref, lhs, cu_ref, ct_ref, xc_ref, w_ref, tb_ref,
     tin_ref, own_ref, sg_ref, shl_ref, d0_ref, u_ref, t_ref,
     k_ref, ku_ref, fw_ref, ft_ref, gw_ref, dw_ref, rf_ref, rd_ref, re_ref, ea_ref,
     loc_sem, x_s, x_r, f_s, f_r, fo_s, fo_r, g_s, g_r, go_s, go_r,
-    lb_s, lb_r, xl_s, xl_r, xo_s, xo_r, y0_s, y0_r, x0_s, x0_r,
+    y0_s, y0_r, x0_s, x0_r,
     tt_s, tt_r, own_sem, y_s, y_r, yo_s, yo_r, z_s, z_r, o_s, o_r, b_s, b_r,
     keep_sem, a_s, a_r, sf_s, sf_r, sd_s, sd_r, sg_s, se_s, se_r,
 ):
@@ -129,12 +129,10 @@
     zs = [spot(x, y, mod4(z + d), c) for d in (1, -1)]
     poles = [lax.rem(p + d, 8) for d in range(8)]
     grids = [lax.rem(g + d, 16) for d in range(1, 16)]
-    beyond = (partner[0], over[1])
+    peers = [[spot(mod4(x + d), y, z, cc) for cc in (c, 1 - c)] for d in range(4)]
     hs_ref[0] = h_ref[...]
     hs_ref[1] = s_ref[...]
-    greet(
-        [(pp, g) for pp in poles[1:]] + [(pp, sib) for pp in poles[1:]] + [(p, gg) for gg in grids] + [beyond]
-    )
+    greet([peers[d][e] for d in range(4) for e in (0, 1) if d + e > 0] + ys + zs)
 
     pending = []
 
@@ -156,26 +154,15 @@
         yy, zz = jnp.where(first, f, s), jnp.where(first, s, f)
         return pl.multiple_of(slot * 512 + lax.rem(yy, 2) * 256 + (2 * zz + half(yy)) * 32, 32)
 
-    def quarter(xx):
-        return pl.ds(pl.multiple_of(xx * 128, 128), 128)
-
     def slab(slot, f, s):
-        rows = pl.ds(row(slot, f, s), 32)
-        return ab_ref.at[:, rows, :] if slot < 2 else ab_ref.at[:, rows, quarter(x)]
+        return ab_ref.at[:, pl.ds(row(slot, f, s), 32), :]
 
     def part(slot, f, s, k):
-        rows = pl.ds(row(slot, f, s), 32)
-        return ab_ref.at[k, rows, :] if slot < 2 else ab_ref.at[k, rows, quarter(x)]
-
-    def own_slab(slot):
-        return slab(slot, f0, g0) if slot < 2 else lb_ref.at[:, yl, :, quarter(x)]
+        return ab_ref.at[k, pl.ds(row(slot, f, s), 32), :]
 
     root = x >= 2
-    peers = [[spot(mod4(x + d), y, z, cc) for cc in (c, 1 - c)] for d in range(4)]
 
     def land(slot, cc):
-        if slot == 2:
-            return lb_ref.at[:, yl, pl.ds(pl.multiple_of(cc * 16, 16), 16), :]
         return ab_ref.at[:, pl.ds(pl.multiple_of(slot * 512 + yl * 256 + q * 32 + cc * 16, 16), 16), :]
 
     def child_cols(k):
@@ -198,7 +185,7 @@
             (jnp.logical_and(x < 2, x != c), [], [give(0, d, 1) for d in range(4)]),
         ]
 
-    gifts = givers(2) + givers(0) + givers(1)
+    gifts = givers(0) + givers(1) + givers(2)
     for when, here, away in gifts:
 
         @pl.when(when)
@@ -207,7 +194,7 @@
                 copy.start()
 
     def taken(slot):
-        source = c if slot == 0 else slot + 1
+        source = jnp.where(slot == 0, c, slot + 1)
         remote(land(slot, 1 - c), land(slot, 1 - c), x_s.at[1, 1], x_r.at[slot, 1], peers[1][1]).wait_recv()
 
         @pl.when(x != source)
@@ -240,15 +227,15 @@
     g_at = (mod4(g0 - 1), mod4(g0 + 1), mod4(g0 + 2))
 
     def spread(slot, n):
-        dst = slab(slot, f_at[n], g0)
-        ref = own_slab(slot) if n == 0 else dst
+        ref = slab(slot, f_at[n], g0)
         for d in (0, 1):
-            go(remote(ref, dst, g_s.at[d, slot, n], g_r.at[d, slot, n], gs[d]))
+            go(remote(ref, ref, g_s.at[d, slot, n], g_r.at[d, slot, n], gs[d]))
 
     def open_slot(slot):
         taken(slot)
         for d in (0, 1):
-            go(remote(own_slab(slot), slab(slot, f0, g0), f_s.at[d, slot], f_r.at[d, slot], fs[d]))
+            ref = slab(slot, f0, g0)
+            go(remote(ref, ref, f_s.at[d, slot], f_r.at[d, slot], fs[d]))
         spread(slot, 0)
 
     def near(slot):
@@ -277,41 +264,6 @@
             for d in (0, 1):
                 ref = part(slot, f_at[n], g_at[2], d)
                 remote(ref, ref, go_s.at[slot, n, d], go_r.at[slot, n, d], gs[d]).wait_recv()
-
-    def last_rows():
-        ref = lb_ref.at[:, yl]
-        go(remote(ref, ref, lb_s, lb_r, partner))
-        pltpu.make_async_copy(own_slab(2), slab(2, f0, g0), loc_sem.at[5]).start()
-
-    def last_rows_in():
-        ref = lb_ref.at[:, 1 - yl]
-        remote(ref, ref, lb_s, lb_r, partner).wait_recv()
-
-    xx_at = (mod4(x - 1), mod4(x + 1), mod4(x + 2))
-    along = (peers[1][0], peers[3][0])
-
-    def column(xx):
-        return ab_ref.at[:, pl.ds(1024, 512), quarter(xx)]
-
-    def column_part(xx, k):
-        return ab_ref.at[k, pl.ds(1024, 512), quarter(xx)]
-
-    def join():
-        pltpu.make_async_copy(own_slab(2), slab(2, f0, g0), loc_sem.at[5]).wait()
-        for d in (0, 1):
-            go(remote(column(x), column(x), xl_s.at[d], xl_r.at[d], along[d]))
-
-    def join_more():
-        for d in (0, 1):
-            ref = column(xx_at[d])
-            remote(ref, ref, xl_s.at[d], xl_r.at[d], along[d]).wait_recv()
-            ref = column_part(xx_at[d], d)
-            go(remote(ref, ref, xo_s.at[d], xo_r.at[d], along[d]))
-
-    def join_end():
-        for d in (0, 1):
-            ref = column_part(xx_at[2], d)
-            remote(ref, ref, xo_s.at[d], xo_r.at[d], along[d]).wait_recv()
 
     def top_start():
         @pl.when(root)
@@ -367,11 +319,8 @@
 
     def chain_start():
         for j in range(4):
-            if j < 2:
-                rows = pl.ds(pl.multiple_of(C + j * 256 + q * 32, 32), 32)
-                re, im = couple(ab_ref[0, rows, :], ab_ref[1, rows, :], j)
-            else:
-                re, im = couple(lb_ref[0, j - 2], lb_ref[1, j - 2], j)
+            rows = pl.ds(pl.multiple_of(C + j * 256 + q * 32, 32), 32)
+            re, im = couple(ab_ref[0, rows, :], ab_ref[1, rows, :], j)
             ct_ref[0, j * 32 : j * 32 + 32, :] = re
             ct_ref[1, j * 32 : j * 32 + 32, :] = im
         times(lhs, ehl_ref, cu_ref, ct_ref[0, 0:128, :], ct_ref[1, 0:128, :], C)
@@ -395,34 +344,42 @@
         lr, li = rotate(cu_ref[0] + ct_ref[0], cu_ref[1] + ct_ref[1], dinv_ref[0:1, :], dinv_ref[1:2, :])
         xc_ref[0] = lr[128:192]
         xc_ref[1] = li[128:192]
-        put_pair(lhs, lr, li)
+        put_pair(lhs, lr[0:128], li[0:128])
+        put_pair(lhs, lr[128:192], li[128:192], 512)
 
     def product(n):
         rows = slice(n * 256, n * 256 + 256)
-        wide = dot_t(lhs[0:768, 0 : 2 * C], bhl_ref[0, rows, :])
-        narrow = dot_t(lhs[0:384, 0 : 2 * C], bhl_ref[1, rows, :])
-        pair = fold(wide, narrow, 192)
+        wide = dot_t(lhs[0:512, 0 : 2 * C], bhl_ref[0, rows, :])
+        narrow = dot_t(lhs[0:256, 0 : 2 * C], bhl_ref[1, rows, :])
+        pair = fold(wide, narrow, 128)
         for k in (0, 1):
-            w_ref[k, :, rows] = pair[k][128:192]
             for b, (j, other) in enumerate(BLOCKS):
                 if other == n:
                     for cc in (0, 1):
                         tb_ref[cc, b, k] = pair[k][j * 32 + cc * 16 : j * 32 + cc * 16 + 16]
 
+    def product_w(n):
+        rows = slice(n * 256, n * 256 + 256)
+        wide = dot_t(lhs[512:768, 0 : 2 * C], bhl_ref[0, rows, :])
+        narrow = dot_t(lhs[512:640, 0 : 2 * C], bhl_ref[1, rows, :])
+        w_ref[0, :, rows], w_ref[1, :, rows] = fold(wide, narrow, 64)
+
+    order = (jnp.maximum(x - 1, 0), jnp.where(x < 2, 1, 0), jnp.where(x == 3, 1, 2))
+
+    def turn(stage, o, *more):
+        return lambda: stage(order[o], *more)
+
     steps = [
-        lambda: open_slot(2), last_rows, lambda: open_slot(0), lambda: open_slot(1), top_start,
-        lambda: near(2), lambda: relay(2, 0), lambda: near(0), lambda: far(2),
-        lambda: relay(2, 1), lambda: relay(2, 2), lambda: near(1), lambda: relay(0, 0),
-        lambda: relay(2, 3), lambda: far(0), lambda: close_slot(2), join, top_more,
-        lambda: relay(1, 0), lambda: relay(0, 1), lambda: relay(0, 2), lambda: far(1),
-        lambda: relay(0, 3), lambda: relay(1, 1), last_rows_in, lambda: close_slot(0),
-        lambda: scale_rows(0), lambda: scale_rows(1), lambda: relay(1, 2),
-        lambda: scale_rows(2), lambda: scale_rows(3), lambda: scale_rows(4), join_more,
-        lambda: scale_rows(5), lambda: scale_rows(6), lambda: scale_rows(7), lambda: relay(1, 3),
-        chain_start, chain_two, chain_three, lambda: close_slot(1),
-    ] + [lambda n=n: split_rows(n) for n in range(8)] + [
-        lambda: product(0), lambda: product(1), join_end,
-    ] + [lambda n=n: split_rows(n) for n in range(8, 16)]
+        turn(open_slot, 0), turn(near, 0), turn(relay, 0, 0), turn(far, 0),
+        turn(open_slot, 1), turn(open_slot, 2), top_start,
+        turn(relay, 0, 1), turn(relay, 0, 2), turn(near, 1), turn(relay, 0, 3), turn(relay, 1, 0),
+        turn(near, 2), turn(far, 1), turn(relay, 2, 0), turn(relay, 1, 1), turn(relay, 1, 2), top_more,
+        turn(far, 2), turn(relay, 1, 3), turn(close_slot, 0), turn(close_slot, 1),
+        lambda: scale_rows(0), lambda: scale_rows(1), turn(relay, 2, 1),
+        lambda: scale_rows(2), lambda: scale_rows(3), turn(relay, 2, 2),
+        lambda: scale_rows(4), lambda: scale_rows(5), lambda: scale_rows(6), turn(relay, 2, 3),
+        lambda: scale_rows(7), chain_start, chain_two, chain_three, turn(close_slot, 2),
+    ] + [lambda n=n: split_rows(n) for n in range(16)]
     for step in steps:
         step()
 
@@ -445,11 +402,6 @@
         remote(tb_ref.at[1 - c, blocks], tin_ref.at[blocks], tt_s.at[n], tt_r.at[n], sibling)
         for n, blocks in enumerate(GROUPS_DS)
     ]
-    go(swaps[0])
-    product(2)
-    product(3)
-    go(swaps[1])
-
     def finish(n):
         for b in range(GROUPS[n].start, GROUPS[n].stop):
             j, other = BLOCKS[b]
@@ -481,15 +433,19 @@
             go(remote(dst if src is None else src, dst, z_s.at[d, n, o], z_r.at[d, n, o], zs[d]))
 
     keeps = []
-    for n in (0, 1):
+
+    def launch(n):
         finish(n)
         src = own_ref.at[GROUPS_DS[n]]
-        along_z(n, 0, src)
+        if n == 0:
+            along_z(n, 0, src)
         go(remote(src, whole(n, g), y_s.at[n], y_r.at[n], over))
+        if n == 1:
+            along_z(n, 0, src)
         keep = pltpu.make_async_copy(src, whole(n, g), own_sem.at[n])
         keep.start()
         keeps.append(keep)
-        hand(n, 0, 0, lambda k, n=n: own_ref.at[GROUPS_DS[n], k])
+        hand(n, 0, 0, lambda k: own_ref.at[GROUPS_DS[n], k])
 
     def from_over(n):
         ref = whole(n, base[1])
@@ -525,10 +481,22 @@
             remote(ref, ref, yo_s.at[m, k], yo_r.at[m, k], over).wait_recv()
             go(remote(ref, ref, b_s.at[0, m, 1, k], b_r.at[0, m, 1, k], sibling))
 
+    product(0)
+    product(1)
+    go(swaps[0])
+    product(2)
+    launch(0)
+    product(3)
+    go(swaps[1])
+    product_w(0)
+    launch(1)
     from_z(0, 0)
+    product_w(1)
     from_over(1)
     along_z(1, 1, None)
     from_over(0)
+    product_w(2)
+    product_w(3)
     from_far(0, 0)
     from_z(1, 0)
     over_far(1)
@@ -599,7 +567,8 @@
         m = jnp.where(iota((64, 1), 0) < 32, pattern_at(j, 0), pattern_at(j, 1))
         side = weighted[:, cols] * m
         fw_ref[:, cols] = side
-        ft_ref[j] = side.T.reshape(16, 16, 64)
+        turned = side.T.reshape(16, 2, 8, 64)
+        ft_ref[j] = jnp.concatenate([turned[:, 0], turned[:, 1]], axis=2)
 
     for d, gg in enumerate(grids):
         go(remote(ft_ref.at[:, gg], ea_ref.at[g], a_s.at[d], a_r.at[d], (p, gg)))
@@ -688,7 +657,7 @@
             value = value + ref[n]
         return value
 
-    out_ref[:, R : 2 * R] = total(rf_ref)
+    right_ref[...] = total(rf_ref)
 
     @pl.when(lead)
     def _():
@@ -698,16 +667,18 @@
         side = total(re_ref)
         for k in (0, 1):
             for jj in (0, 1):
-                cols = [side[2 * qq + k][:, jj * 32 : jj * 32 + 32] for qq in range(8)]
                 at = k * 512 + jj * 256
-                out_ref[:, at : at + 256] = jnp.concatenate(cols, axis=1)
+                for top_half in (0, 1):
+                    lane = top_half * 64 + jj * 32
+                    cols = [side[2 * qq + k][:, lane : lane + 32] for qq in range(8)]
+                    left_ref[top_half * 8 : top_half * 8 + 8, at : at + 256] = jnp.concatenate(cols, axis=1)
 
     @pl.when(jnp.logical_not(lead))
     def _():
         diag = total(rd_ref)
         upper = p < 2
-        out_ref[:, 0:C] = jnp.where(upper, diag, 0.0)
-        out_ref[:, C : 2 * C] = jnp.where(upper, 0.0, diag)
+        left_ref[:, 0:C] = jnp.where(upper, diag, 0.0)
+        left_ref[:, C : 2 * C] = jnp.where(upper, 0.0, diag)
 
     for copy in pending:
         copy.wait_send()
@@ -731,25 +702,24 @@
 def local(hamiltonian, margin, pattern, shift_real, shift_imag, residue):
     dma = pltpu.SemaphoreType.DMA
     vm = pltpu.VMEM
-    return pl.pallas_call(
+    left, right = pl.pallas_call(
         kernel,
         name="selected_inversion",
-        out_shape=jax.ShapeDtypeStruct((16, 2 * R), F32),
+        out_shape=(jax.ShapeDtypeStruct((16, R), F32), jax.ShapeDtypeStruct((16, R), F32)),
         in_specs=[VM, VM, SM, SM, SM, SM],
-        out_specs=VM,
+        out_specs=(VM, VM),
         scratch_shapes=[
-            vm((2, 16, 2 * R), F32), vm((2, 1536, 512), F32), vm((2, 2, 32, 512), F32), vm((2, 64, 1024), F32), vm((2, 1024, C), BF16), vm((2, R, 2 * C), BF16),
+            vm((2, 16, 2 * R), F32), vm((2, 1536, 512), F32), vm((2, 64, 1024), F32), vm((2, 1024, C), BF16), vm((2, R, 2 * C), BF16),
             vm((8, C), F32), vm((768, 2 * R), BF16), vm((2, 192, C), F32), vm((2, 192, C), F32),
             vm((2, 64, C), F32), vm((2, 64, R), F32), vm((2, NB, 2, 16, 256), F32),
             vm((NB, 2, 16, 256), F32), vm((NB, 2, 16, 256), F32), vm((NB, 2, 16, 16, 256), F32),
             vm((2, 2 * R, R), BF16), vm((8, R), F32), vm((2, 128, R), F32), vm((2, 128, R), F32),
-            vm((2, 64, C), F32), vm((2, 64, C), F32), vm((64, R), F32), vm((4, 16, 16, 64), F32),
+            vm((2, 64, C), F32), vm((2, 64, C), F32), vm((64, R), F32), vm((4, 16, 8, 128), F32),
             vm((64, R), F32), vm((64, C), F32),
-            vm((8, 16, R), F32), vm((8, 16, C), F32), vm((8, 16, 16, 64), F32), vm((16, 4, 16, 64), F32),
-            dma((6,)), dma((4, 2)), dma((3, 2)),
+            vm((8, 16, R), F32), vm((8, 16, C), F32), vm((8, 16, 8, 128), F32), vm((16, 4, 8, 128), F32),
+            dma((5,)), dma((4, 2)), dma((3, 2)),
             dma((2, 3)), dma((2, 3)), dma((3, 2)), dma((3, 2)),
             dma((2, 3, 4)), dma((2, 3, 4)), dma((3, 4, 2)), dma((3, 4, 2)),
-            dma, dma, dma((2,)), dma((2,)), dma((2,)), dma((2,)),
             dma((2,)), dma((2,)), dma((3, 2, 2)), dma((2, 2, 2)),
             dma((2,)), dma((2,)), dma((2,)), dma((2,)), dma((2,)), dma((4, 2)), dma((4, 2)),
             dma((2, 2, 2)), dma((2, 2, 2)), dma((2, 2, 2)), dma((2, 2, 2)),
@@ -762,6 +732,7 @@
         ),
         cost_estimate=pl.CostEstimate(flops=12 << 30, bytes_accessed=1 << 20, transcendentals=0),
     )(hamiltonian, margin, pattern, shift_real, shift_imag, residue)
+    return jnp.concatenate([left, right], axis=1)
 
 
 def solution(mesh):

time: 129 us -> 110 us (0.85)
  Pallas kernels: 126 us -> 107 us
  local copies, waits for them, and re-layouts: 1.57 us -> 0 us
  other arithmetic: 0 us -> 1.54 us
    pallas_call x1, Pallas kernels: 126 us -> 107 us  [local(): pl.pallas_call(kernel, name='selected_inversion', out_shape=(jax.ShapeDty...]
    unnamed x1 -> x0, local copies, waits for them, and re-layouts: 1.57 us -> none
    concatenate x0 -> x1, other arithmetic: none -> 1.54 us  [local(): return jnp.concatenate([left, right], axis=1)]
where the time goes in v4:
time: 110 us
  Pallas kernels  107 us (97%)
  other arithmetic  1.54 us (1%)
  between operations  1.31 us (1%)
    pallas_call x1, Pallas kernels, local(): pl.pallas_call(kernel, name='selected_inversion', out_shape=(jax.ShapeDty...  107 us

profile of v4, /device:TPU:1, one launch (start us, length us, event | category | flops | bytes accessed | tf_op | source)
XLA Modules:
  0.0 109.8 jit_solution(15852284565238894996)
XLA Ops:
  1.3 107.0 %selected_inversion.1 = (f32[16,1024]{1,0:T(8,128)}, f32[16,1024]{1,0:T(8,128)}) custom-call(f32[16,2048]{1,0:T(8,128)} %h_ref.1, f32[16,2048]{1,0:T(8,128)} %s_ref.1, s32[4,4]{1,0:T(4,128)} %pat_ref.1, f32[1]{0:T(128)S(6)} %copy.7.sr_ref, f32[1]{0:T(128)S(6)} %copy.8.si_ref, f32[1,2]{1,0:T(1,128)} %res_ref.1), custom_call_target="tpu_custom_call" | custom-call | flops 12884901888 | bytes 1048576 | tf_op jit(solution)/shard_map/selected_inversion/pallas_call | solution.py:705
  108.3 1.5 %pad_maximum_fusion = f32[16,2048]{1,0:T(8,128)} fusion(f32[16,1024]{1,0:T(8,128)} %get-tuple-element.8, f32[16,1024]{1,0:T(8,128)} %get-tuple-element.7), kind=kLoop, calls=%fused_computation | loop fusion | flops 32768 | bytes 262144 | tf_op jit(solution)/shard_map/concatenate | solution.py:735

commit v5 on v4

--- a/solution.py
+++ b/solution.py
@@ -10,6 +10,7 @@
 F32 = jnp.float32
 BF16 = jnp.bfloat16
 MESH = pl.DeviceIdType.MESH
+ANY = pl.BlockSpec(memory_space=pl.ANY)
 VM = pl.BlockSpec(memory_space=pltpu.VMEM)
 SM = pl.BlockSpec(memory_space=pltpu.SMEM)
 BLOCKS = ((0, 0), (3, 0), (0, 1), (1, 1), (0, 2), (1, 2), (2, 2), (1, 3), (2, 3), (3, 3))
@@ -110,11 +111,11 @@
     h_ref, s_ref, pat_ref, sr_ref, si_ref, res_ref, left_ref, right_ref,
     hs_ref, ab_ref, a0_ref, ehl_ref, bhl_ref, dinv_ref, lhs, cu_ref, ct_ref, xc_ref, w_ref, tb_ref,
     tin_ref, own_ref, sg_ref, shl_ref, d0_ref, u_ref, t_ref,
-    k_ref, ku_ref, fw_ref, ft_ref, gw_ref, dw_ref, rf_ref, rd_ref, re_ref, ea_ref,
+    k_ref, ku_ref, fw_ref, ft_ref, gw_ref, dw_ref, rf_ref, rd_ref, re_ref, ea_ref, pre_ref, pin_ref,
     loc_sem, x_s, x_r, f_s, f_r, fo_s, fo_r, g_s, g_r, go_s, go_r,
     y0_s, y0_r, x0_s, x0_r,
     tt_s, tt_r, own_sem, y_s, y_r, yo_s, yo_r, z_s, z_r, o_s, o_r, b_s, b_r,
-    keep_sem, a_s, a_r, sf_s, sf_r, sd_s, sd_r, sg_s, se_s, se_r,
+    pre_s, pre_r, keep_sem, a_s, a_r, sf_s, sf_r, sd_s, sd_r, sg_s, se_s, se_r,
 ):
     p, g, x, yl, z, yh, q, c = place()
     y = 2 * yh + yl
@@ -130,10 +131,13 @@
     poles = [lax.rem(p + d, 8) for d in range(8)]
     grids = [lax.rem(g + d, 16) for d in range(1, 16)]
     peers = [[spot(mod4(x + d), y, z, cc) for cc in (c, 1 - c)] for d in range(4)]
-    hs_ref[0] = h_ref[...]
-    hs_ref[1] = s_ref[...]
+    loads = [pltpu.make_async_copy(ref, hs_ref.at[k], loc_sem.at[k]) for k, ref in enumerate((h_ref, s_ref))]
+    for copy in loads:
+        copy.start()
     greet([peers[d][e] for d in range(4) for e in (0, 1) if d + e > 0] + ys + zs)
 
+    for copy in loads:
+        copy.wait()
     pending = []
 
     def go(copy):
@@ -178,20 +182,28 @@
 
     def givers(slot):
         if slot > 0:
-            away = [give(slot, d, e) for d in range(4) for e in (0, 1) if d + e > 0]
-            return [(x == slot + 1, [stay_put(slot)], away)]
+            away = [give(slot, d, e) for d, e in ((0, 1), (1, 0), (3, 0), (1, 1), (3, 1))]
+            return [(x == slot + 1, [stay_put(slot)], away, [give(slot, 2, e) for e in (0, 1)])]
         return [
-            (jnp.logical_and(x < 2, x == c), [stay_put(0)], [give(0, d, 0) for d in (1, 2, 3)]),
-            (jnp.logical_and(x < 2, x != c), [], [give(0, d, 1) for d in range(4)]),
+            (jnp.logical_and(x < 2, x == c), [stay_put(0)], [give(0, d, 0) for d in (1, 3)], [give(0, 2, 0)]),
+            (jnp.logical_and(x < 2, x != c), [], [give(0, d, 1) for d in (0, 1, 3)], [give(0, 2, 1)]),
         ]
 
     gifts = givers(0) + givers(1) + givers(2)
-    for when, here, away in gifts:
+    for when, here, away, opposite in gifts:
 
         @pl.when(when)
         def _():
             for copy in away + here:
                 copy.start()
+
+    def give_opposite():
+        for when, here, away, opposite in gifts:
+
+            @pl.when(when)
+            def _():
+                for copy in opposite:
+                    copy.start()
 
     def taken(slot):
         source = jnp.where(slot == 0, c, slot + 1)
@@ -370,7 +382,7 @@
         return lambda: stage(order[o], *more)
 
     steps = [
-        turn(open_slot, 0), turn(near, 0), turn(relay, 0, 0), turn(far, 0),
+        turn(open_slot, 0), give_opposite, turn(near, 0), turn(relay, 0, 0), turn(far, 0),
         turn(open_slot, 1), turn(open_slot, 2), top_start,
         turn(relay, 0, 1), turn(relay, 0, 2), turn(near, 1), turn(relay, 0, 3), turn(relay, 1, 0),
         turn(near, 2), turn(far, 1), turn(relay, 2, 0), turn(relay, 1, 1), turn(relay, 1, 2), top_more,
@@ -505,45 +517,65 @@
     from_far(1, 0)
     over_far(3)
     from_far(1, 1)
-    for n in (0, 1):
+
+    def arrived(n):
         for m in range(4):
             for o in (0, 1):
                 gg = base[o] + hop[m] + 1 - 2 * c
                 for k in (0, 1):
                     ref = piece(n, gg, k)
                     remote(ref, ref, b_s.at[n, m, o, k], b_r.at[n, m, o, k], sibling).wait_recv()
-    for keep in keeps:
-        keep.wait()
+        keeps[n].wait()
 
     def block(b, k):
         return sg_ref[b, k].reshape(256, 256)
 
     eye = iota((256, 256), 1) == iota((256, 256), 0)
-    for j in range(4):
-        rows = slice(j * 256, j * 256 + 256)
-        low = slice(R + j * 256, R + j * 256 + 256)
+    inverse = {}
+
+    def diagonal(j):
         b = WHERE[(j, j)]
         ir, ii = recip(
             jnp.sum(jnp.where(eye, block(b, 0), 0.0), axis=1, keepdims=True),
             jnp.sum(jnp.where(eye, block(b, 1), 0.0), axis=1, keepdims=True),
         )
-        d0_ref[0:1, rows] = jnp.sum(jnp.where(eye, ir, 0.0), axis=0, keepdims=True)
-        d0_ref[1:2, rows] = jnp.sum(jnp.where(eye, ii, 0.0), axis=0, keepdims=True)
+        cols = slice(j * 256, j * 256 + 256)
+        d0_ref[0:1, cols] = jnp.sum(jnp.where(eye, ir, 0.0), axis=0, keepdims=True)
+        d0_ref[1:2, cols] = jnp.sum(jnp.where(eye, ii, 0.0), axis=0, keepdims=True)
+        inverse[j] = ir, ii
+
+    def scale_block(j, other):
+        rows = slice(j * 256, j * 256 + 256)
+        low = slice(R + j * 256, R + j * 256 + 256)
+        cols = slice(other * 256, other * 256 + 256)
+        if (j, other) in WHERE:
+            b = WHERE[(j, other)]
+            re, im = block(b, 0), block(b, 1)
+        else:
+            b = WHERE[(other, j)]
+            re, im = block(b, 0).T, block(b, 1).T
+        ir, ii = inverse[j]
+        er, ei = rotate(re, im, -ir, -ii)
+        for where, value in ((rows, er), (low, ei)):
+            if j == other:
+                value = jnp.where(eye, 0.0, value)
+            high, rest = split(value)
+            shl_ref[0, where, cols] = high
+            shl_ref[1, where, cols] = rest
+
+    early = ((0, 0), (0, 1), (0, 3), (1, 0), (1, 1))
+    arrived(0)
+    diagonal(0)
+    diagonal(1)
+    for pair in early:
+        scale_block(*pair)
+    arrived(1)
+    diagonal(2)
+    diagonal(3)
+    for j in range(4):
         for other in range(4):
-            cols = slice(other * 256, other * 256 + 256)
-            if (j, other) in WHERE:
-                b = WHERE[(j, other)]
-                re, im = block(b, 0), block(b, 1)
-            else:
-                b = WHERE[(other, j)]
-                re, im = block(b, 0).T, block(b, 1).T
-            er, ei = rotate(re, im, -ir, -ii)
-            for where, value in ((rows, er), (low, ei)):
-                if j == other:
-                    value = jnp.where(eye, 0.0, value)
-                high, rest = split(value)
-                shl_ref[0, where, cols] = high
-                shl_ref[1, where, cols] = rest
+            if (j, other) not in early:
+                scale_block(j, other)
     times(lhs, shl_ref, u_ref, w_ref[0], w_ref[1], R)
     u_ref[0, 0:64, :] += w_ref[0]
     u_ref[1, 0:64, :] += w_ref[1]
@@ -590,16 +622,26 @@
 
         sent.append((here, away, stay))
 
-    def child_rows(src, dst, ss, rs):
+    def child_rows():
         for jj in (0, 1):
             for cc in (0, 1):
                 here = jnp.logical_and(p == 2 * c + jj, c == cc)
                 rows = pl.ds(jj * 32 + cc * 16, 16)
-                send_or_keep(src.at[rows, :], dst.at[p], ss.at[jj, cc], rs.at[p], (2 * c + jj, 2 * q + cc), here)
+                send_or_keep(
+                    dw_ref.at[rows, :], rd_ref.at[p], sd_s.at[jj, cc], sd_r.at[p], (2 * c + jj, 2 * q + cc), here
+                )
 
     for j in range(4):
-        send_or_keep(gw_ref.at[pl.ds(j * 16, 16), :], rf_ref.at[p], sg_s.at[j], sf_r.at[p], (4 + j, g), p == 4 + j)
-    child_rows(fw_ref, rf_ref, sf_s, sf_r)
+        xx = 2 + j // 2
+        send_or_keep(
+            gw_ref.at[pl.ds(j * 16, 16), :], rf_ref.at[x, j % 2], sg_s.at[j], sf_r.at[x, j % 2], (2 * xx + yl, g), x == xx
+        )
+    for jj in (0, 1):
+        for cc in (0, 1):
+            send_or_keep(
+                fw_ref.at[pl.ds(jj * 32 + cc * 16, 16), :], rf_ref.at[x, jj], sf_s.at[jj, cc], sf_r.at[x, jj],
+                (2 * c + yl, 2 * q + cc), jnp.logical_and(x == c, c == cc),
+            )
 
     rh, rl = split(yr)
     ih, il = split(yi)
@@ -626,13 +668,9 @@
     times(lhs, ehl_ref, k_ref, k_ref[0], k_ref[1], C)
     zr, zi = rotate(ku_ref[0] + k_ref[0], ku_ref[1] + k_ref[1], dinv_ref[0:1, :], dinv_ref[1:2, :])
     dw_ref[...] = wr * (xc_ref[0] + zr) - wi * (xc_ref[1] + zi)
-    child_rows(dw_ref, rd_ref, sd_s, sd_r)
+    child_rows()
 
     for here, away, stay in sent:
-
-        @pl.when(jnp.logical_not(here))
-        def _():
-            away.wait_send()
 
         @pl.when(here)
         def _():
@@ -640,12 +678,19 @@
 
     lead = p >= 4
     same = jnp.logical_or(lead, c == half(p))
+    for d in range(4):
+        xx = mod4(x + d)
+
+        @pl.when(jnp.logical_or(jnp.logical_not(same), d > 0))
+        def _():
+            for n in (0, 1):
+                remote(rf_ref.at[xx, n], rf_ref.at[xx, n], sf_s.at[0, 0], sf_r.at[xx, n], partner).wait_recv()
+
+    pre_ref[...] = rf_ref[0, 1 - yl] + rf_ref[1, 1 - yl] + rf_ref[2, 1 - yl] + rf_ref[3, 1 - yl]
+    cross = remote(pre_ref, pin_ref, pre_s, pre_r, partner)
+    go(cross)
     for d in range(8):
         pp = poles[d]
-
-        @pl.when(jnp.logical_or(jnp.logical_not(same), d > 0))
-        def _():
-            remote(rf_ref.at[pp], rf_ref.at[pp], sf_s.at[0, 0], sf_r.at[pp], partner).wait_recv()
 
         @pl.when(jnp.logical_and(jnp.logical_not(lead), jnp.logical_or(jnp.logical_not(same), d > 0)))
         def _():
@@ -656,8 +701,6 @@
         for n in range(1, 8):
             value = value + ref[n]
         return value
-
-    right_ref[...] = total(rf_ref)
 
     @pl.when(lead)
     def _():
@@ -680,14 +723,24 @@
         left_ref[:, 0:C] = jnp.where(upper, diag, 0.0)
         left_ref[:, C : 2 * C] = jnp.where(upper, 0.0, diag)
 
+    main = rf_ref[0, yl] + rf_ref[1, yl] + rf_ref[2, yl] + rf_ref[3, yl]
+    cross.wait_recv()
+    right_ref[...] = main + pin_ref[...]
+
+    for here, away, stay in sent:
+
+        @pl.when(jnp.logical_not(here))
+        def _():
+            away.wait_send()
+
     for copy in pending:
         copy.wait_send()
 
-    for when, here, away in gifts:
+    for when, here, away, opposite in gifts:
 
         @pl.when(when)
         def _():
-            for copy in away:
+            for copy in away + opposite:
                 copy.wait_send()
 
     @pl.when(root)
@@ -706,7 +759,7 @@
         kernel,
         name="selected_inversion",
         out_shape=(jax.ShapeDtypeStruct((16, R), F32), jax.ShapeDtypeStruct((16, R), F32)),
-        in_specs=[VM, VM, SM, SM, SM, SM],
+        in_specs=[ANY, ANY, SM, SM, SM, SM],
         out_specs=(VM, VM),
         scratch_shapes=[
             vm((2, 16, 2 * R), F32), vm((2, 1536, 512), F32), vm((2, 64, 1024), F32), vm((2, 1024, C), BF16), vm((2, R, 2 * C), BF16),
@@ -716,7 +769,8 @@
             vm((2, 2 * R, R), BF16), vm((8, R), F32), vm((2, 128, R), F32), vm((2, 128, R), F32),
             vm((2, 64, C), F32), vm((2, 64, C), F32), vm((64, R), F32), vm((4, 16, 8, 128), F32),
             vm((64, R), F32), vm((64, C), F32),
-            vm((8, 16, R), F32), vm((8, 16, C), F32), vm((8, 16, 8, 128), F32), vm((16, 4, 8, 128), F32),
+            vm((4, 2, 16, R), F32), vm((8, 16, C), F32), vm((8, 16, 8, 128), F32), vm((16, 4, 8, 128), F32),
+            vm((16, R), F32), vm((16, R), F32),
             dma((5,)), dma((4, 2)), dma((3, 2)),
             dma((2, 3)), dma((2, 3)), dma((3, 2)), dma((3, 2)),
             dma((2, 3, 4)), dma((2, 3, 4)), dma((3, 4, 2)), dma((3, 4, 2)),
@@ -724,7 +778,7 @@
             dma((2,)), dma((2,)), dma((2,)), dma((2,)), dma((2,)), dma((4, 2)), dma((4, 2)),
             dma((2, 2, 2)), dma((2, 2, 2)), dma((2, 2, 2)), dma((2, 2, 2)),
             dma((2, 4, 2, 2)), dma((2, 4, 2, 2)),
-            dma, dma((15,)), dma((15,)), dma((2, 2)), dma((8,)), dma((2, 2)), dma((8,)),
+            dma, dma, dma, dma((15,)), dma((15,)), dma((2, 2)), dma((4, 2)), dma((2, 2)), dma((8,)),
             dma((4,)), dma((4,)), dma((8,)),
         ],
         compiler_params=pltpu.CompilerParams(

time: 110 us -> 107 us (0.973)
  Pallas kernels: 107 us -> 104 us
    pallas_call x1, Pallas kernels: 107 us -> 104 us  [local(): pl.pallas_call(kernel, name='selected_inversion', out_shape=(jax.ShapeDty...]
where the time goes in v5:
time: 107 us; the launch traced here: 106 us
  Pallas kernels  104 us (97%)
  other arithmetic  1.54 us (1%)
  between operations  1.31 us (1%)
    pallas_call x1, Pallas kernels, local(): pl.pallas_call(kernel, name='selected_inversion', out_shape=(jax.ShapeDty...  104 us

profile of v5, /device:TPU:1, one launch (start us, length us, event | category | flops | bytes accessed | tf_op | source)
XLA Modules:
  0.0 106.4 jit_solution(1376218919090066716)
XLA Ops:
  1.3 103.6 %selected_inversion.1 = (f32[16,1024]{1,0:T(8,128)}, f32[16,1024]{1,0:T(8,128)}) custom-call(f32[16,2048]{1,0:T(8,128)} %h_ref.1, f32[16,2048]{1,0:T(8,128)} %s_ref.1, s32[4,4]{1,0:T(4,128)} %pat_ref.1, f32[1]{0:T(128)S(6)} %copy.7.sr_ref, f32[1]{0:T(128)S(6)} %copy.8.si_ref, f32[1,2]{1,0:T(1,128)} %res_ref.1), custom_call_target="tpu_custom_call" | custom-call | flops 12884901888 | bytes 1048576 | tf_op jit(solution)/shard_map/selected_inversion/pallas_call | solution.py:758
  104.9 1.5 %pad_maximum_fusion = f32[16,2048]{1,0:T(8,128)} fusion(f32[16,1024]{1,0:T(8,128)} %get-tuple-element.8, f32[16,1024]{1,0:T(8,128)} %get-tuple-element.7), kind=kLoop, calls=%fused_computation | loop fusion | flops 32768 | bytes 262144 | tf_op jit(solution)/shard_map/concatenate | solution.py:789

commit v6 on v5

--- a/solution.py
+++ b/solution.py
@@ -589,10 +589,12 @@
         u_ref[0, rows, :] = jnp.where(on, 1.0, er)
         u_ref[1, rows, :] = ei
     times(lhs, shl_ref, t_ref, u_ref[0], u_ref[1], R)
-    times(lhs, shl_ref, t_ref, t_ref[0], t_ref[1], R)
-    yr, yi = rotate(u_ref[0] + t_ref[0], u_ref[1] + t_ref[1], d0_ref[0:1, :], d0_ref[1:2, :])
-    gw_ref[...] = wr * yr[64:128] - wi * yi[64:128]
-    yr, yi = yr[0:64], yi[0:64]
+    times(lhs, shl_ref, t_ref, t_ref[0, 0:64], t_ref[1, 0:64], R)
+    yr, yi = rotate(
+        u_ref[0, 0:64] + t_ref[0, 0:64], u_ref[1, 0:64] + t_ref[1, 0:64], d0_ref[0:1, :], d0_ref[1:2, :]
+    )
+    u_ref[0, 0:64, :] = yr
+    u_ref[1, 0:64, :] = yi
     weighted = -(wr * yr - wi * yi)
     for j in range(4):
         cols = slice(j * 256, j * 256 + 256)
@@ -631,11 +633,6 @@
                     dw_ref.at[rows, :], rd_ref.at[p], sd_s.at[jj, cc], sd_r.at[p], (2 * c + jj, 2 * q + cc), here
                 )
 
-    for j in range(4):
-        xx = 2 + j // 2
-        send_or_keep(
-            gw_ref.at[pl.ds(j * 16, 16), :], rf_ref.at[x, j % 2], sg_s.at[j], sf_r.at[x, j % 2], (2 * xx + yl, g), x == xx
-        )
     for jj in (0, 1):
         for cc in (0, 1):
             send_or_keep(
@@ -643,6 +640,25 @@
                 (2 * c + yl, 2 * q + cc), jnp.logical_and(x == c, c == cc),
             )
 
+    times(lhs, shl_ref, t_ref, t_ref[0, 64:128], t_ref[1, 64:128], R)
+    gr, gi = rotate(
+        u_ref[0, 64:128] + t_ref[0, 0:64], u_ref[1, 64:128] + t_ref[1, 0:64], d0_ref[0:1, :], d0_ref[1:2, :]
+    )
+    gw_ref[...] = wr * gr - wi * gi
+    for j in range(4):
+        xx = 2 + j // 2
+        send_or_keep(
+            gw_ref.at[pl.ds(j * 16, 16), :], rf_ref.at[x, j % 2], sg_s.at[j], sf_r.at[x, j % 2], (2 * xx + yl, g), x == xx
+        )
+
+    keep.wait()
+    for d in range(15):
+        gg = lax.rem(g + 15 - d, 16)
+        remote(ea_ref.at[gg], ea_ref.at[gg], a_s.at[d], a_r.at[d], (p, grids[0])).wait_recv()
+    for j in range(4):
+        send_or_keep(ea_ref.at[:, j], re_ref.at[p], se_s.at[j], se_r.at[p], (4 + j, g), p == 4 + j)
+
+    yr, yi = u_ref[0, 0:64, :], u_ref[1, 0:64, :]
     rh, rl = split(yr)
     ih, il = split(yi)
     for at, (re, im) in enumerate(((rh, ih), (rl, il))):
@@ -653,13 +669,6 @@
     wide = dot(lhs[0:256, 0:R], bhl_ref[0, :, 0:C]) + dot(lhs[0:256, R : 2 * R], bhl_ref[0, :, C : 2 * C])
     narrow = dot(lhs[0:128, 0:R], bhl_ref[1, :, 0:C]) + dot(lhs[0:128, R : 2 * R], bhl_ref[1, :, C : 2 * C])
     pr, pi = fold(wide, narrow, 64)
-
-    keep.wait()
-    for d in range(15):
-        gg = lax.rem(g + 15 - d, 16)
-        remote(ea_ref.at[gg], ea_ref.at[gg], a_s.at[d], a_r.at[d], (p, grids[0])).wait_recv()
-    for j in range(4):
-        send_or_keep(ea_ref.at[:, j], re_ref.at[p], se_s.at[j], se_r.at[p], (4 + j, g), p == 4 + j)
 
     times(lhs, ehl_ref, k_ref, pr, pi, C)
     ku_ref[0] = k_ref[0] + pr

time: 107 us -> 106 us (level)
  no operation moved by 1% of the time
where the time goes in v6:
time: 106 us
  Pallas kernels  103 us (97%)
  other arithmetic  1.54 us (1%)
  between operations  1.31 us (1%)
    pallas_call x1, Pallas kernels, local(): pl.pallas_call(kernel, name='selected_inversion', out_shape=(jax.ShapeDty...  103 us

profile of v6, /device:TPU:1, one launch (start us, length us, event | category | flops | bytes accessed | tf_op | source)
XLA Modules:
  0.0 105.6 jit_solution(16359361948986509255)
XLA Ops:
  1.3 102.8 %selected_inversion.1 = (f32[16,1024]{1,0:T(8,128)}, f32[16,1024]{1,0:T(8,128)}) custom-call(f32[16,2048]{1,0:T(8,128)} %h_ref.1, f32[16,2048]{1,0:T(8,128)} %s_ref.1, s32[4,4]{1,0:T(4,128)} %pat_ref.1, f32[1]{0:T(128)S(6)} %copy.7.sr_ref, f32[1]{0:T(128)S(6)} %copy.8.si_ref, f32[1,2]{1,0:T(1,128)} %res_ref.1), custom_call_target="tpu_custom_call" | custom-call | flops 12884901888 | bytes 1048576 | tf_op jit(solution)/shard_map/selected_inversion/pallas_call | solution.py:767
  104.1 1.5 %pad_maximum_fusion = f32[16,2048]{1,0:T(8,128)} fusion(f32[16,1024]{1,0:T(8,128)} %get-tuple-element.8, f32[16,1024]{1,0:T(8,128)} %get-tuple-element.7), kind=kLoop, calls=%fused_computation | loop fusion | flops 32768 | bytes 262144 | tf_op jit(solution)/shard_map/concatenate | solution.py:798

commit v7 on v6

--- a/solution.py
+++ b/solution.py
@@ -434,10 +434,9 @@
     base = (g, g + 2 - 4 * yh)
     hop = [0] + [4 * (mod4(z + d) - z) for d in (-1, 1, 2)]
 
-    def hand(n, m, o, ref_of):
-        for k in (0, 1):
-            ref = piece(n, base[o] + hop[m], k)
-            go(remote(ref_of(k), ref, b_s.at[n, m, o, k], b_r.at[n, m, o, k], sibling))
+    def hand(n, m, o, src=None):
+        dst = whole(n, base[o] + hop[m])
+        go(remote(dst if src is None else src, dst, b_s.at[n, m, o, 0], b_r.at[n, m, o, 0], sibling))
 
     def along_z(n, o, src):
         dst = whole(n, base[o])
@@ -457,12 +456,12 @@
         keep = pltpu.make_async_copy(src, whole(n, g), own_sem.at[n])
         keep.start()
         keeps.append(keep)
-        hand(n, 0, 0, lambda k: own_ref.at[GROUPS_DS[n], k])
+        hand(n, 0, 0, src)
 
     def from_over(n):
         ref = whole(n, base[1])
         remote(ref, ref, y_s.at[n], y_r.at[n], over).wait_recv()
-        hand(n, 0, 1, lambda k: piece(n, base[1], k))
+        hand(n, 0, 1)
 
     def from_z(n, o):
         for d in (0, 1):
@@ -472,10 +471,9 @@
             ref = piece(n, gg, d)
             go(remote(ref, ref, o_s.at[n, o, d], o_r.at[n, o, d], zs[d]))
             if n == 0:
-                for k in (0, 1):
-                    ref = piece(n, gg, k)
-                    go(remote(ref, ref, yo_s.at[1 + d, k], yo_r.at[1 + d, k], over))
-            hand(n, 1 + d, o, lambda k, gg=gg: piece(n, gg, k))
+                ref = whole(n, gg)
+                go(remote(ref, ref, yo_s.at[1 + d, 0], yo_r.at[1 + d, 0], over))
+            hand(n, 1 + d, o)
 
     def from_far(n, o):
         gg = base[o] + hop[3]
@@ -488,6 +486,11 @@
 
     def over_far(m):
         gg = base[1] + hop[m]
+        if m < 3:
+            ref = whole(0, gg)
+            remote(ref, ref, yo_s.at[m, 0], yo_r.at[m, 0], over).wait_recv()
+            hand(0, m, 1)
+            return
         for k in (0, 1):
             ref = piece(0, gg, k)
             remote(ref, ref, yo_s.at[m, k], yo_r.at[m, k], over).wait_recv()
@@ -522,8 +525,8 @@
         for m in range(4):
             for o in (0, 1):
                 gg = base[o] + hop[m] + 1 - 2 * c
-                for k in (0, 1):
-                    ref = piece(n, gg, k)
+                for k in (0, 1) if m == 3 else (0,):
+                    ref = piece(n, gg, k) if m == 3 else whole(n, gg)
                     remote(ref, ref, b_s.at[n, m, o, k], b_r.at[n, m, o, k], sibling).wait_recv()
         keeps[n].wait()
 

time: 106 us -> 106 us (level)
  no operation moved by 1% of the time
where the time goes in v7:
time: 106 us
  Pallas kernels  103 us (97%)
  other arithmetic  1.54 us (1%)
  between operations  1.31 us (1%)
    pallas_call x1, Pallas kernels, local(): pl.pallas_call(kernel, name='selected_inversion', out_shape=(jax.ShapeDty...  103 us

profile of v7, /device:TPU:1, one launch (start us, length us, event | category | flops | bytes accessed | tf_op | source)
XLA Modules:
  0.0 105.5 jit_solution(11721737024391101584)
XLA Ops:
  1.3 102.7 %selected_inversion.1 = (f32[16,1024]{1,0:T(8,128)}, f32[16,1024]{1,0:T(8,128)}) custom-call(f32[16,2048]{1,0:T(8,128)} %h_ref.1, f32[16,2048]{1,0:T(8,128)} %s_ref.1, s32[4,4]{1,0:T(4,128)} %pat_ref.1, f32[1]{0:T(128)S(6)} %copy.7.sr_ref, f32[1]{0:T(128)S(6)} %copy.8.si_ref, f32[1,2]{1,0:T(1,128)} %res_ref.1), custom_call_target="tpu_custom_call" | custom-call | flops 12884901888 | bytes 1048576 | tf_op jit(solution)/shard_map/selected_inversion/pallas_call | solution.py:770
  104.0 1.5 %pad_maximum_fusion = f32[16,2048]{1,0:T(8,128)} fusion(f32[16,1024]{1,0:T(8,128)} %get-tuple-element.8, f32[16,1024]{1,0:T(8,128)} %get-tuple-element.7), kind=kLoop, calls=%fused_computation | loop fusion | flops 32768 | bytes 262144 | tf_op jit(solution)/shard_map/concatenate | solution.py:801
